TPU v7x, 32 devices: a whole 2x2x4 slice. The times are simulated.
32 devices in a mesh: groups: 2 (over y), front: 4 (over z), batch: 2 (over x), line: 2 (over core).
Axes of the slice: x: 2, y: 2, z: 4, core: 2. Of those that a mesh axis runs over, the one named last changes fastest.
Arguments:
- injections: float32 [2048, 512], P('front', ('groups', 'batch')), parts along dimension 1, may hold values from -6 to 6
- switch_from: int32 [2, 512], P(None, ('groups', 'batch')), parts along dimension 1, may hold values from 0 to 2047
- switch_to: int32 [2, 512], P(None, ('groups', 'batch')), parts along dimension 1, may hold values from 0 to 2047
- switch_susc: float32 [2, 512], P(None, ('groups', 'batch')), parts along dimension 1, may hold values from 0.5 to 4
- coupling: float32 [2048, 512], P('front'), may hold values from -1 to 1
- pivot_inverse: float32 [2048, 512], P('front')
- branch_from: int32 [4096], P(('front', 'line')), may hold values from 0 to 2047, as said below
- branch_to: int32 [4096], P(('front', 'line')), may hold values from 0 to 2047, as said below
- branch_susc: float32 [4096], P(('front', 'line')), may hold values from 0.5 to 2
- branch_owner: int32 [4096, 1], P(('front', 'line')), may hold values from 0 to 7; in each aligned block of 512 rows (0 to 511, 512 to 1023, ...) at most 128 rows name the same one
- in_weight: float32 [128], replicated, may hold values from -4 to 4
- in_bias: float32 [128], replicated, may hold values from -1 to 1
- out_weight: bfloat16 [128, 128], replicated, may hold values from -0.5 to 0.5
Outputs:
- region_scores: bfloat16 [8, 512, 128], P(('front', 'line'), ('groups', 'batch')), parts along dimension 1
- angles: float32 [2048, 512], P('front', ('groups', 'batch')), parts along dimension 1
There are 2 independent parts, one for each index of `groups`. A program takes and returns all parts, laid end to end along the dimension named above; an argument that names none is the same for every part. Nothing has to cross between parts.
Inputs may be any that keep to these rules, and one draw needn't show every extreme that they name: `branch_from`: the bus of row r lies in slab s = r // 1024, between s * 512 and s * 512 + 511. `branch_to`: the bus of row r lies in slab s = r // 1024 or in slab s + 1. `branch_owner`: in each aligned block of 512 rows (the branches of one device) no owner is named by more than 128 rows.
All inputs are finite; a program needn't handle non-finite values.
Results may differ from a plain program's by a relative error of at most 0.005.
Values sent between devices are 32-bit elements; how exact they have to be, the bound alone decides.
A program may use at most 64 MiB of HBM per device.

v0:
```python
import jax
import jax.numpy as jnp
from jax import lax
from jax.sharding import PartitionSpec as P

K = 2
BR_DEV = 512


def from_behind(value, axis, by):
    count = lax.axis_size(axis)
    pairs = [(i, i + by) for i in range(count) if 0 <= i + by < count]
    return lax.ppermute(value, axis, pairs)


def product(operand, against):
    return jnp.dot(
        operand, against, precision=lax.Precision.HIGHEST, preferred_element_type=jnp.float32
    )


def centered_tanh(loadings, in_weight, in_bias):
    return jnp.tanh(loadings[..., None] * in_weight + in_bias) - jnp.tanh(in_bias)


def capacitance_solve(terms, switch_susc):
    switches = switch_susc.shape[0]
    factor = [[None] * switches for row_at in range(switches)]
    for row_at in range(switches):
        for col_at in range(row_at + 1):
            partial_sum = terms[row_at, 1 + col_at]
            if row_at == col_at:
                partial_sum = partial_sum + 1.0 / switch_susc[row_at]
            for inner_at in range(col_at):
                partial_sum = partial_sum - factor[row_at][inner_at] * factor[col_at][inner_at]
            if row_at == col_at:
                factor[row_at][col_at] = jnp.sqrt(partial_sum)
            else:
                factor[row_at][col_at] = partial_sum / factor[col_at][col_at]
    lower_part = []
    for row_at in range(switches):
        running = terms[row_at, 0]
        for inner_at in range(row_at):
            running = running - factor[row_at][inner_at] * lower_part[inner_at]
        lower_part.append(running / factor[row_at][row_at])
    weights = [None] * switches
    for row_at in reversed(range(switches)):
        running = lower_part[row_at]
        for inner_at in range(row_at + 1, switches):
            running = running - factor[inner_at][row_at] * weights[inner_at]
        weights[row_at] = running / factor[row_at][row_at]
    return jnp.stack(weights)


def body(
    injections,
    switch_from,
    switch_to,
    switch_susc,
    coupling,
    pivot_inverse,
    branch_from,
    branch_to,
    branch_susc,
    branch_owner,
    in_weight,
    in_bias,
    out_weight,
):
    fronts = lax.axis_size("front")
    front_at = lax.axis_index("front")
    slab_size = coupling.shape[1]
    topo_count = injections.shape[1]
    first_bus = front_at * slab_size
    bus_ids = first_bus + jnp.arange(slab_size, dtype=jnp.int32)
    from_hot = (bus_ids[:, None, None] == switch_from[None]).astype(jnp.float32)
    to_hot = (bus_ids[:, None, None] == switch_to[None]).astype(jnp.float32)
    incidence = from_hot - to_hot
    stacked = jnp.concatenate([injections[:, None, :], incidence], axis=1).reshape(slab_size, -1)

    def lower_step(step_at, current):
        arrived = from_behind(current, "front", 1)
        return stacked - product(coupling, arrived)

    lowered = lax.fori_loop(0, fronts - 1, lower_step, stacked)
    pivoted = product(pivot_inverse, lowered)

    def upper_step(step_at, current):
        arrived = from_behind(product(coupling.T, current), "front", -1)
        return pivoted - arrived

    solved = lax.fori_loop(0, fronts - 1, upper_step, pivoted)
    solved_cols = solved.reshape(slab_size, K + 1, topo_count)
    local_terms = jnp.einsum(
        "bit,bct->ict", incidence, solved_cols, precision=lax.Precision.HIGHEST
    )
    terms = lax.psum(local_terms, "front")
    weights = capacitance_solve(terms, switch_susc)
    angles = solved_cols[:, 0, :] - jnp.einsum(
        "bit,it->bt", solved_cols[:, 1:, :], weights, precision=lax.Precision.HIGHEST
    )
    following = from_behind(angles, "front", -1)
    joined = jnp.concatenate([angles, following], axis=0)
    flows = branch_susc[:, None] * (joined[branch_from - first_bus] - joined[branch_to - first_bus])
    owners = lax.axis_size(("front", "line"))
    capacity = 2 * BR_DEV // owners
    owner_ids = branch_owner[:, 0]
    owner_hot = (owner_ids[:, None] == jnp.arange(owners, dtype=jnp.int32)[None]).astype(jnp.int32)
    before = jnp.cumsum(owner_hot, axis=0) - owner_hot
    position = jnp.sum(before * owner_hot, axis=1)
    slot_ids = owner_ids * capacity + position
    dispatch = (jnp.arange(owners * capacity, dtype=jnp.int32)[:, None] == slot_ids[None]).astype(
        jnp.float32
    )
    outgoing = product(dispatch, flows).reshape(owners, capacity, topo_count)
    arrived = lax.all_to_all(outgoing, ("front", "line"), split_axis=0, concat_axis=0, tiled=True)
    slot_rows = arrived.reshape(-1, arrived.shape[2])
    span_size = 32
    blocks = slot_rows.reshape(-1, span_size, slot_rows.shape[1])

    def accumulate(running, slot_block):
        return (running + jnp.sum(centered_tanh(slot_block, in_weight, in_bias), axis=0), None)

    start_sum = jnp.zeros((slot_rows.shape[1], in_weight.shape[0]), jnp.float32)
    summed, unused = lax.scan(accumulate, start_sum, blocks)
    pooled = (summed * BR_DEV ** (-0.5)).astype(jnp.bfloat16)
    region_scores = jnp.dot(pooled, out_weight, preferred_element_type=jnp.float32).astype(
        jnp.bfloat16
    )
    return (region_scores[None], angles)


def solution(mesh):
    in_specs = (
        P("front", ("groups", "batch")),
        P(None, ("groups", "batch")),
        P(None, ("groups", "batch")),
        P(None, ("groups", "batch")),
        P("front", None),
        P("front", None),
        P(("front", "line")),
        P(("front", "line")),
        P(("front", "line")),
        P(("front", "line"), None),
        P(),
        P(),
        P(),
    )
    out_specs = (P(("front", "line"), ("groups", "batch"), None), P("front", ("groups", "batch")))
    return jax.shard_map(body, mesh=mesh, in_specs=in_specs, out_specs=out_specs, check_vma=False)
```

profile of v0, /device:TPU:0, one launch (start us, length us, event | category | flops | bytes accessed | tf_op | source)
XLA Modules:
  0.0 243.3 jit_solution(18174583019754320143)
XLA Ops:
  0.7 1.2 copy.31
  1.8 0.8 convert_subtract_fusion
  3.0 0.9 copy.53
  4.5 73.9 %while.32 = (s32[]{:T(128)}, f32[512,384]{1,0:T(8,128)}, f32[512,512]{1,0:T(8,128)S(1)}, f32[512,384]{1,0:T(8,128)S(1)}, s32[]{:T(128)}) while((s32[]{:T(128)}, f32[512,384]{1,0:T(8,128)}, f32[512,512]{1,0:T(8,128)S(1)}, f32[512,384]{1,0:T(8,128)S(1)}, s32[]{:T(128)}) %tuple.77), condition=%wide.region_4.0_spmd, body=%wide.region_3.0_spmd.sunk | while | flops 1208156160 | bytes 6553701 | solution.py:85
  4.5 5.8 %collective-permute-start = (f32[512,384]{1,0:T(8,128)}, f32[512,384]{1,0:T(8,128)}, u32[]{:S(2)}, u32[]{:S(2)}) collective-permute-start(f32[512,384]{1,0:T(8,128)} %get-tuple-element.274), channel_id=1, source_target_pairs={{0,4},{4,8},{8,12},{1,5},{5,9},{9,13},{2,6},{6,10},{10,14},{3,7},{... | collective-permute-start | bytes 2359304 | tf_op jit(solution)/shard_map/while/body/eval_jaxpr/ppermute | solution.py:13
  10.3 16.2 %collective-permute-done = f32[512,384]{1,0:T(8,128)} collective-permute-done((f32[512,384]{1,0:T(8,128)}, f32[512,384]{1,0:T(8,128)}, u32[]{:S(2)}, u32[]{:S(2)}) %collective-permute-start) | collective-permute-done | bytes 786464 | tf_op jit(solution)/shard_map/while/body/eval_jaxpr/ppermute | solution.py:13
  26.6 3.8 %convolution_subtract_fusion.2 = f32[512,384]{1,0:T(8,128)} fusion(f32[512,384]{1,0:T(8,128)S(1)} %get-tuple-element.281, f32[512,512]{1,0:T(8,128)S(1)} %get-tuple-element.280, f32[512,384]{1,0:T(8,128)} %collective-permute-done), kind=kOutput, calls=%fused_computation.2.clone.1 | convolution fusion | flops 1208156160 | bytes 3407872 | tf_op jit(solution)/shard_map/while/body/eval_jaxpr/dot_general | solution.py:17
  30.4 5.3 %collective-permute-start = (f32[512,384]{1,0:T(8,128)}, f32[512,384]{1,0:T(8,128)}, u32[]{:S(2)}, u32[]{:S(2)}) collective-permute-start(f32[512,384]{1,0:T(8,128)} %get-tuple-element.274), channel_id=1, source_target_pairs={{0,4},{4,8},{8,12},{1,5},{5,9},{9,13},{2,6},{6,10},{10,14},{3,7},{... | collective-permute-start | bytes 2359304 | tf_op jit(solution)/shard_map/while/body/eval_jaxpr/ppermute | solution.py:13
  35.7 15.4 %collective-permute-done = f32[512,384]{1,0:T(8,128)} collective-permute-done((f32[512,384]{1,0:T(8,128)}, f32[512,384]{1,0:T(8,128)}, u32[]{:S(2)}, u32[]{:S(2)}) %collective-permute-start) | collective-permute-done | bytes 786464 | tf_op jit(solution)/shard_map/while/body/eval_jaxpr/ppermute | solution.py:13
  51.0 3.8 %convolution_subtract_fusion.2 = f32[512,384]{1,0:T(8,128)} fusion(f32[512,384]{1,0:T(8,128)S(1)} %get-tuple-element.281, f32[512,512]{1,0:T(8,128)S(1)} %get-tuple-element.280, f32[512,384]{1,0:T(8,128)} %collective-permute-done), kind=kOutput, calls=%fused_computation.2.clone.1 | convolution fusion | flops 1208156160 | bytes 3407872 | tf_op jit(solution)/shard_map/while/body/eval_jaxpr/dot_general | solution.py:17
  54.9 5.3 %collective-permute-start = (f32[512,384]{1,0:T(8,128)}, f32[512,384]{1,0:T(8,128)}, u32[]{:S(2)}, u32[]{:S(2)}) collective-permute-start(f32[512,384]{1,0:T(8,128)} %get-tuple-element.274), channel_id=1, source_target_pairs={{0,4},{4,8},{8,12},{1,5},{5,9},{9,13},{2,6},{6,10},{10,14},{3,7},{... | collective-permute-start | bytes 2359304 | tf_op jit(solution)/shard_map/while/body/eval_jaxpr/ppermute | solution.py:13
  60.1 14.4 %collective-permute-done = f32[512,384]{1,0:T(8,128)} collective-permute-done((f32[512,384]{1,0:T(8,128)}, f32[512,384]{1,0:T(8,128)}, u32[]{:S(2)}, u32[]{:S(2)}) %collective-permute-start) | collective-permute-done | bytes 786464 | tf_op jit(solution)/shard_map/while/body/eval_jaxpr/ppermute | solution.py:13
  74.5 3.8 %convolution_subtract_fusion.2 = f32[512,384]{1,0:T(8,128)} fusion(f32[512,384]{1,0:T(8,128)S(1)} %get-tuple-element.281, f32[512,512]{1,0:T(8,128)S(1)} %get-tuple-element.280, f32[512,384]{1,0:T(8,128)} %collective-permute-done), kind=kOutput, calls=%fused_computation.2.clone.1 | convolution fusion | flops 1208156160 | bytes 3407872 | tf_op jit(solution)/shard_map/while/body/eval_jaxpr/dot_general | solution.py:17
  78.4 4.7 %convolution_bitcast_fusion = f32[512,384]{0,1:T(8,128)} fusion(f32[512,384]{1,0:T(8,128)} %get-tuple-element.98, f32[512,512]{1,0:T(8,128)S(1)} %copy-done), kind=kOutput, calls=%fused_computation.8 | convolution fusion | flops 1207959552 | bytes 2621440 | tf_op jit(solution)/shard_map/dot_general | solution.py:17
  83.1 1.4 copy.34
  84.5 0.9 copy.59
  85.4 72.7 %while.33 = (s32[]{:T(128)}, f32[512,384]{1,0:T(8,128)}, f32[512,512]{1,0:T(8,128)S(1)}, f32[512,384]{1,0:T(8,128)S(1)}, s32[]{:T(128)}) while((s32[]{:T(128)}, f32[512,384]{1,0:T(8,128)}, f32[512,512]{1,0:T(8,128)S(1)}, f32[512,384]{1,0:T(8,128)S(1)}, s32[]{:T(128)}) %tuple.78), condition=%wide.region_6.7_spmd, body=%wide.region_5.0_spmd.sunk | while | flops 1208156160 | bytes 8126565 | solution.py:92
  85.4 3.8 %fusion.37 = f32[512,384]{1,0:T(8,128)} fusion(f32[512,512]{1,0:T(8,128)S(1)} %get-tuple-element.295, f32[512,384]{1,0:T(8,128)} %get-tuple-element.289), kind=kOutput, calls=%fused_computation.57.clone.1 | convolution fusion | flops 1207959552 | bytes 2621440 | tf_op jit(solution)/shard_map/while/body/eval_jaxpr/dot_general | solution.py:17
  89.2 1.3 collective-permute-start.1
  90.5 18.2 %collective-permute-done.1 = f32[512,384]{1,0:T(8,128)} collective-permute-done((f32[512,384]{1,0:T(8,128)}, f32[512,384]{1,0:T(8,128)}, u32[]{:S(2)}, u32[]{:S(2)}) %collective-permute-start.1) | collective-permute-done | bytes 786464 | tf_op jit(solution)/shard_map/while/body/eval_jaxpr/ppermute | solution.py:13
  108.7 2.1 sub.95
  110.8 3.8 %fusion.37 = f32[512,384]{1,0:T(8,128)} fusion(f32[512,512]{1,0:T(8,128)S(1)} %get-tuple-element.295, f32[512,384]{1,0:T(8,128)} %get-tuple-element.289), kind=kOutput, calls=%fused_computation.57.clone.1 | convolution fusion | flops 1207959552 | bytes 2621440 | tf_op jit(solution)/shard_map/while/body/eval_jaxpr/dot_general | solution.py:17
  114.7 1.3 collective-permute-start.1
  116.0 16.8 %collective-permute-done.1 = f32[512,384]{1,0:T(8,128)} collective-permute-done((f32[512,384]{1,0:T(8,128)}, f32[512,384]{1,0:T(8,128)}, u32[]{:S(2)}, u32[]{:S(2)}) %collective-permute-start.1) | collective-permute-done | bytes 786464 | tf_op jit(solution)/shard_map/while/body/eval_jaxpr/ppermute | solution.py:13
  132.8 2.1 sub.95
  134.9 3.8 %fusion.37 = f32[512,384]{1,0:T(8,128)} fusion(f32[512,512]{1,0:T(8,128)S(1)} %get-tuple-element.295, f32[512,384]{1,0:T(8,128)} %get-tuple-element.289), kind=kOutput, calls=%fused_computation.57.clone.1 | convolution fusion | flops 1207959552 | bytes 2621440 | tf_op jit(solution)/shard_map/while/body/eval_jaxpr/dot_general | solution.py:17
  138.7 1.3 collective-permute-start.1
  140.0 15.9 %collective-permute-done.1 = f32[512,384]{1,0:T(8,128)} collective-permute-done((f32[512,384]{1,0:T(8,128)}, f32[512,384]{1,0:T(8,128)}, u32[]{:S(2)}, u32[]{:S(2)}) %collective-permute-start.1) | collective-permute-done | bytes 786464 | tf_op jit(solution)/shard_map/while/body/eval_jaxpr/ppermute | solution.py:13
  155.9 2.1 sub.95
  158.0 1.4 copy.36
  159.4 4.5 %convolution_bitcast_fusion.1 = f32[2,3,128]{1,0,2:T(2,128)S(1)} fusion(f32[512,3,128]{0,2,1:T(8,128)S(1)} %bitcast.81, f32[512,2,128]{0,2,1:T(8,128)S(1)} %convert_subtract_fusion), kind=kOutput, calls=%fused_computation.9 | convolution fusion | flops 4718592 | bytes 1313792 | tf_op jit(solution)/shard_map/bit,bct->ict/dot_general | solution.py:94
  163.9 19.6 %psum.7 = f32[2,3,128]{1,0,2:T(2,128)S(1)} all-reduce(f32[2,3,128]{1,0,2:T(2,128)S(1)} %convolution_bitcast_fusion.1), channel_id=1, replica_groups=mesh['groups'=2,'front'=4,'batch'=2,'line'=2] {'front'}, use_global_device_ids=true, to_apply=%region_7.8 | all-reduce | flops 768 | bytes 6144 | tf_op jit(solution)/shard_map/psum | solution.py:97
  183.5 2.2 slice_reduce_fusion.2
  186.2 1.3 collective-permute-start.2
  187.6 1.1 reduce-window.6
  189.1 5.4 %collective-permute-done.2 = f32[512,128]{1,0:T(8,128)S(1)} collective-permute-done((f32[512,128]{1,0:T(8,128)S(1)}, f32[512,128]{1,0:T(8,128)S(1)}, u32[]{:S(2)}, u32[]{:S(2)}) %collective-permute-start.2) | collective-permute-done | bytes 262176 | tf_op jit(solution)/shard_map/ppermute | solution.py:13
  194.5 1.0 gather_fusion.1
  195.6 1.0 gather_fusion
  196.7 1.9 fusion
  198.6 3.5 %all-to-all-start = ((f32[8,128,128]{2,1,0:T(8,128)}), f32[8,128,128]{2,1,0:T(8,128)S(1)}, u32[]{:S(2)}, u32[]{:S(2)}) async-start(f32[8,128,128]{2,1,0:T(8,128)} %bitcast.13), calls=%async_computation | async-start | bytes 1048576 | tf_op jit(solution)/shard_map/all_to_all | solution.py:116
  202.1 15.2 %all-to-all-done = f32[8,128,128]{2,1,0:T(8,128)S(1)} async-done(((f32[8,128,128]{2,1,0:T(8,128)}), f32[8,128,128]{2,1,0:T(8,128)S(1)}, u32[]{:S(2)}, u32[]{:S(2)}) %all-to-all-start) | async-done | bytes 524320 | tf_op jit(solution)/shard_map/all_to_all | solution.py:116
  217.4 25.2 %while.34 = (s32[]{:T(128)}, f32[128,128]{1,0:T(8,128)S(1)}, f32[32,32,128]{2,1,0:T(8,128)S(1)}, f32[128]{0:T(128)S(1)}, f32[128]{0:T(128)S(1)}, /*index=5*/f32[1,1,128]{2,1,0:T(1,128)S(1)}, s32[]{:T(128)}, s32[]{:T(128)}) while((s32[]{:T(128)}, f32[128,128]{1,0:T(8,128)S(1)}, f32[32,32,128]{2,1,0:T(8,128)S(1)}, ...), condition=%wide.region_10.11_spmd.clone, body=%wide.region_8.10_spmd.clone.sunk | while | flops 2113539 | bytes 312931 | solution.py:125
  217.4 0.7 subtract_reduce_fusion.2
  218.2 0.7 subtract_reduce_fusion.2
  219.0 0.7 subtract_reduce_fusion.2
  219.8 0.7 subtract_reduce_fusion.2
  220.6 0.7 subtract_reduce_fusion.2
  221.3 0.7 subtract_reduce_fusion.2
  222.1 0.7 subtract_reduce_fusion.2
  222.9 0.7 subtract_reduce_fusion.2
  223.7 0.7 subtract_reduce_fusion.2
  224.5 0.7 subtract_reduce_fusion.2
  225.3 0.7 subtract_reduce_fusion.2
  226.1 0.7 subtract_reduce_fusion.2
  226.9 0.7 subtract_reduce_fusion.2
  227.6 0.7 subtract_reduce_fusion.2
  228.4 0.7 subtract_reduce_fusion.2
  230.0 0.7 subtract_reduce_fusion.2
  232.4 0.7 subtract_reduce_fusion.2
  233.9 0.7 subtract_reduce_fusion.2
  235.5 0.7 subtract_reduce_fusion.2
  237.9 0.7 subtract_reduce_fusion.2
  239.4 0.7 subtract_reduce_fusion.2
  242.6 0.8 fusion.1
  (120 shorter events, 10.6 us)
Async XLA Ops:
  0.6 77.8 %copy-start = (f32[512,512]{1,0:T(8,128)S(1)}, f32[512,512]{1,0:T(8,128)}, u32[]{:S(2)}) copy-start(f32[512,512]{1,0:T(8,128)} %param.24) | copy-start | bytes 3145732
  3.0 1.5 copy-start.1
  4.5 22.0 %collective-permute-start = (f32[512,384]{1,0:T(8,128)}, f32[512,384]{1,0:T(8,128)}, u32[]{:S(2)}, u32[]{:S(2)}) collective-permute-start(f32[512,384]{1,0:T(8,128)} %get-tuple-element.274), channel_id=1, source_target_pairs={{0,4},{4,8},{8,12},{1,5},{5,9},{9,13},{2,6},{6,10},{10,14},{3,7},{... | collective-permute-start | bytes 2359304 | tf_op jit(solution)/shard_map/while/body/eval_jaxpr/ppermute | solution.py:13
  30.4 20.6 %collective-permute-start = (f32[512,384]{1,0:T(8,128)}, f32[512,384]{1,0:T(8,128)}, u32[]{:S(2)}, u32[]{:S(2)}) collective-permute-start(f32[512,384]{1,0:T(8,128)} %get-tuple-element.274), channel_id=1, source_target_pairs={{0,4},{4,8},{8,12},{1,5},{5,9},{9,13},{2,6},{6,10},{10,14},{3,7},{... | collective-permute-start | bytes 2359304 | tf_op jit(solution)/shard_map/while/body/eval_jaxpr/ppermute | solution.py:13
  54.9 19.7 %collective-permute-start = (f32[512,384]{1,0:T(8,128)}, f32[512,384]{1,0:T(8,128)}, u32[]{:S(2)}, u32[]{:S(2)}) collective-permute-start(f32[512,384]{1,0:T(8,128)} %get-tuple-element.274), channel_id=1, source_target_pairs={{0,4},{4,8},{8,12},{1,5},{5,9},{9,13},{2,6},{6,10},{10,14},{3,7},{... | collective-permute-start | bytes 2359304 | tf_op jit(solution)/shard_map/while/body/eval_jaxpr/ppermute | solution.py:13
  89.2 19.5 %collective-permute-start.1 = (f32[512,384]{1,0:T(8,128)}, f32[512,384]{1,0:T(8,128)}, u32[]{:S(2)}, u32[]{:S(2)}) collective-permute-start(f32[512,384]{1,0:T(8,128)} %fusion.37), channel_id=1, source_target_pairs={{4,0},{8,4},{12,8},{5,1},{9,5},{13,9},{6,2},{10,6},{14,10},{7,3},{... | collective-permute-start | bytes 2359304 | tf_op jit(solution)/shard_map/while/body/eval_jaxpr/ppermute | solution.py:13
  114.7 18.1 %collective-permute-start.1 = (f32[512,384]{1,0:T(8,128)}, f32[512,384]{1,0:T(8,128)}, u32[]{:S(2)}, u32[]{:S(2)}) collective-permute-start(f32[512,384]{1,0:T(8,128)} %fusion.37), channel_id=1, source_target_pairs={{4,0},{8,4},{12,8},{5,1},{9,5},{13,9},{6,2},{10,6},{14,10},{7,3},{... | collective-permute-start | bytes 2359304 | tf_op jit(solution)/shard_map/while/body/eval_jaxpr/ppermute | solution.py:13
  138.7 17.2 %collective-permute-start.1 = (f32[512,384]{1,0:T(8,128)}, f32[512,384]{1,0:T(8,128)}, u32[]{:S(2)}, u32[]{:S(2)}) collective-permute-start(f32[512,384]{1,0:T(8,128)} %fusion.37), channel_id=1, source_target_pairs={{4,0},{8,4},{12,8},{5,1},{9,5},{13,9},{6,2},{10,6},{14,10},{7,3},{... | collective-permute-start | bytes 2359304 | tf_op jit(solution)/shard_map/while/body/eval_jaxpr/ppermute | solution.py:13
  163.9 21.8 %copy-start.8 = (f32[2,128]{1,0:T(2,128)S(1)}, f32[2,128]{1,0:T(2,128)}, u32[]{:S(2)}) copy-start(f32[2,128]{1,0:T(2,128)} %param.22) | copy-start | bytes 3076
  185.9 1.7 copy-start.6
  185.9 1.7 copy-start.7
  185.9 1.7 copy-start.4
  186.2 9.4 %copy-start.2 = (f32[512,128]{1,0:T(8,128)}, f32[512,128]{1,0:T(8,128)S(1)}, u32[]{:S(2)}) copy-start(f32[512,128]{1,0:T(8,128)S(1)} %bitcast_subtract_fusion) | copy-start | bytes 786436
  186.2 8.3 %collective-permute-start.2 = (f32[512,128]{1,0:T(8,128)S(1)}, f32[512,128]{1,0:T(8,128)S(1)}, u32[]{:S(2)}, u32[]{:S(2)}) collective-permute-start(f32[512,128]{1,0:T(8,128)S(1)} %bitcast_subtract_fusion), channel_id=1, source_target_pairs={{4,0},{8,4},{12,8},{5,1},{9,5},{13,9},{6,2},{10,6},{14,10},{7,3},{... | collective-permute-start | bytes 786440 | tf_op jit(solution)/shard_map/ppermute | solution.py:13
  195.6 1.1 copy-start.5
  196.7 5.5 %copy-start.10 = (f32[128]{0:T(128)S(1)}, f32[128]{0:T(128)}, u32[]{:S(2)}) copy-start(f32[128]{0:T(128)} %param.30) | copy-start | bytes 1540
  196.7 20.7 %copy-start.9 = (f32[128]{0:T(128)S(1)}, f32[128]{0:T(128)}, u32[]{:S(2)}) copy-start(f32[128]{0:T(128)} %param.29) | copy-start | bytes 1540
  198.6 18.8 %all-to-all-start = ((f32[8,128,128]{2,1,0:T(8,128)}), f32[8,128,128]{2,1,0:T(8,128)S(1)}, u32[]{:S(2)}, u32[]{:S(2)}) async-start(f32[8,128,128]{2,1,0:T(8,128)} %bitcast.13), calls=%async_computation | async-start | bytes 1048576 | tf_op jit(solution)/shard_map/all_to_all | solution.py:116
  217.4 25.2 %copy-start.3 = (bf16[128,128]{1,0:T(8,128)(2,1)S(1)}, bf16[128,128]{1,0:T(8,128)(2,1)}, u32[]{:S(2)}) copy-start(bf16[128,128]{1,0:T(8,128)(2,1)} %param.31) | copy-start | bytes 98308
where the time goes:
time: 244 us; the launch traced here: 243 us
  waiting for transfers between devices  118 us (48%)
  matrix products  34.9 us (14%)
  other arithmetic  32.3 us (13%)
  starting transfers between devices  24.9 us (10%)
  blocking collectives  19.6 us (8%)
  local copies, waits for them, and re-layouts  11.7 us (5%)
    ppermute x7, waiting for transfers between devices, from_behind(): return lax.ppermute(value, axis, pairs)  102 us
    dot_general x8, matrix products, product(): jnp.dot(operand, against, precision=lax.Precision.HIGHEST, preferred_elem...  29.7 us
    reduce_sum x32, other arithmetic, accumulate(): jnp.sum(centered_tanh(slot_block, in_weight, in_bias), axis=0)  23 us
    ppermute x7, starting transfers between devices, from_behind(): return lax.ppermute(value, axis, pairs)  21.5 us
    psum x1, blocking collectives, body(): terms = lax.psum(local_terms, 'front')  19.6 us
    all_to_all x1, waiting for transfers between devices, body(): lax.all_to_all(outgoing, ('front', 'line'), split_axis=0, concat_axis=0,...  15.2 us
    sub x3, other arithmetic, upper_step(): return pivoted - arrived  6.31 us
  transfers between devices with their start and end apart: 8, of which 8 were waited for; matrix products, arithmetic and copies ran while one was open for 1% of the time, Pallas kernels for 0%

commit v1 on v0

v1 whole, which is shorter than its diff:
```python
import functools

import jax
import jax.numpy as jnp
from jax import lax
from jax.experimental import pallas as pl
from jax.experimental.pallas import tpu as pltpu
from jax.sharding import PartitionSpec as P

CHUNKS = 4
UNROLL = 8
SCALE = 512 ** (-0.5)
F32, BF16 = jnp.float32, jnp.bfloat16
VMEM_BYTES = 40 * 1024 * 1024


def split(value):
    high = value.astype(BF16)
    return high, (value - high.astype(F32)).astype(BF16)


def dot(operand, against):
    return jnp.dot(operand, against, preferred_element_type=F32)


def product(operand, against):
    high, low = split(operand)
    return dot(high, against[0]) + (dot(low, against[0]) + dot(high, against[1]))


def copy_to(src, dst, send_sem, recv_sem, front, line):
    return pltpu.make_async_remote_copy(
        src_ref=src,
        dst_ref=dst,
        send_sem=send_sem,
        recv_sem=recv_sem,
        device_id={"front": front, "line": line},
        device_id_type=pl.DeviceIdType.MESH,
    )


def greet(front, line):
    pl.semaphore_signal(
        pltpu.get_barrier_semaphore(),
        inc=1,
        device_id={"front": front, "line": line},
        device_id_type=pl.DeviceIdType.MESH,
    )


def capacitance_solve(terms, switch_susc):
    switches = len(switch_susc)
    factor = [[None] * switches for row_at in range(switches)]
    for row_at in range(switches):
        for col_at in range(row_at + 1):
            partial_sum = terms[row_at][1 + col_at]
            if row_at == col_at:
                partial_sum = partial_sum + 1.0 / switch_susc[row_at]
            for inner_at in range(col_at):
                partial_sum = partial_sum - factor[row_at][inner_at] * factor[col_at][inner_at]
            if row_at == col_at:
                factor[row_at][col_at] = jnp.sqrt(partial_sum)
            else:
                factor[row_at][col_at] = partial_sum / factor[col_at][col_at]
    lower_part = []
    for row_at in range(switches):
        running = terms[row_at][0]
        for inner_at in range(row_at):
            running = running - factor[row_at][inner_at] * lower_part[inner_at]
        lower_part.append(running / factor[row_at][row_at])
    weights = [None] * switches
    for row_at in reversed(range(switches)):
        running = lower_part[row_at]
        for inner_at in range(row_at + 1, switches):
            running = running - factor[inner_at][row_at] * weights[inner_at]
        weights[row_at] = running / factor[row_at][row_at]
    return weights


def solve_kernel(
    fronts, inj, sw_from, sw_to, sw_susc, coupling, pivot, joined,
    yown, yrecv, zown, town, trecv, wown, wrecv, cown, crecv, xfull, xnext, injt,
    e_fwd, e_back, p_fwd,
    y_s, y_r, t_s, t_r, w_s, w_r, c_s, c_r, x_s, x_r, n_s, n_r,
):
    me, line = lax.axis_index("front"), lax.axis_index("line")
    other = 1 - line
    first, last = me == 0, me == fronts - 1
    bus, topo = inj.shape
    switches = sw_from.shape[1]
    rows = topo // (2 * CHUNKS)
    kinds = switches + 1
    pairs = [(i, c) for i in range(switches) for c in range(i + 2)]

    greet(me, other)

    @pl.when(jnp.logical_not(first))
    def _():
        greet(me - 1, 0)
        greet(me - 1, 1)

    @pl.when(jnp.logical_not(last))
    def _():
        greet(me + 1, 0)
        greet(me + 1, 1)

    injt[...] = inj[...].T.reshape(injt.shape)

    def stack(c, carry):
        yown[c, 0:rows] = injt[line, c]
        ids = me * bus + lax.broadcasted_iota(jnp.int32, (rows, bus), 1)
        at = pl.ds(pl.multiple_of((line * CHUNKS + c) * rows, rows), rows)
        f, t = sw_from[at, :], sw_to[at, :]
        for i in range(switches):
            yown[c, (1 + i) * rows:(2 + i) * rows] = (ids == f[:, i:i + 1]).astype(F32) - (
                ids == t[:, i:i + 1]
            ).astype(F32)
        return carry

    lax.fori_loop(0, CHUNKS, stack, 0)
    pl.semaphore_wait(
        pltpu.get_barrier_semaphore(),
        1 + 2 * jnp.where(first, 0, 1) + 2 * jnp.where(last, 0, 1),
    )

    def y_copy(c):
        return copy_to(yown.at[c], yrecv.at[c], y_s.at[c], y_r.at[c], me + 1, line)

    def t_copy(c):
        return copy_to(town.at[c], trecv.at[c], t_s.at[c], t_r.at[c], me + 1, line)

    def w_copy(c):
        return copy_to(wown.at[c], wrecv.at[c], w_s.at[c], w_r.at[c], me - 1, line)

    def c_copy(c):
        return copy_to(cown.at[c], crecv.at[c], c_s.at[c], c_r.at[c], me - 1, line)

    def x_copy(c, half):
        place = xfull.at[half, c]
        return copy_to(place, place, x_s.at[c], x_r.at[c], me, other)

    def n_copy(c, half, to):
        return copy_to(
            xfull.at[half, c], xnext.at[half, c], n_s.at[to, c], n_r.at[half, c], me - 1, to
        )

    def each(fn):
        def step(c, carry):
            fn(c)
            return carry

        lax.fori_loop(0, CHUNKS, step, 0)

    @pl.when(first)
    def _():
        each(lambda c: y_copy(c).start())

    e_fwd[0], e_fwd[1] = split(coupling[...].T)
    p_fwd[0], p_fwd[1] = split(pivot[...].T)
    e_back[0], e_back[1] = split(coupling[...])
    lanes = lax.broadcasted_iota(jnp.int32, (rows, 128), 1)

    def back(c):
        w = wown[c]
        x = zown[c, 0:rows]
        for i in range(switches):
            x = x - zown[c, (1 + i) * rows:(2 + i) * rows] * w[:, i:i + 1]
        xfull[line, c] = x

        @pl.when(jnp.logical_not(last))
        def _():
            c_copy(c).wait_recv()
            xfull[line, c] = xfull[line, c] - crecv[c]

        @pl.when(jnp.logical_not(first))
        def _():
            cown[c] = product(xfull[line, c], e_back)
            c_copy(c).start()
            n_copy(c, line, 0).start()
            n_copy(c, line, 1).start()

        x_copy(c, line).start()

    def ahead(c):
        @pl.when(jnp.logical_not(first))
        def _():
            y_copy(c).wait_recv()
            yown[c] = yown[c] - product(yrecv[c], e_fwd)

            @pl.when(jnp.logical_not(last))
            def _():
                y_copy(c).start()

        y = yown[c]
        z = product(y, p_fwd)
        zown[c] = z
        block = jnp.zeros((rows, 128), F32)
        for j, (i, k) in enumerate(pairs):
            term = jnp.sum(
                y[(1 + i) * rows:(2 + i) * rows] * z[k * rows:(k + 1) * rows],
                axis=1, keepdims=True,
            )
            block = jnp.where(lanes == j, term, block)
        town[c] = block

        @pl.when(jnp.logical_not(first))
        def _():
            t_copy(c).wait_recv()
            town[c] = town[c] + trecv[c]

        @pl.when(jnp.logical_not(last))
        def _():
            t_copy(c).start()

        @pl.when(last)
        def _():
            total = town[c]
            terms = [[None] * kinds for i in range(switches)]
            for j, (i, k) in enumerate(pairs):
                terms[i][k] = total[:, j:j + 1]
            at = pl.ds(pl.multiple_of((line * CHUNKS + c) * rows, rows), rows)
            susc = sw_susc[at, :]
            weights = capacitance_solve(terms, [susc[:, i:i + 1] for i in range(switches)])
            w = jnp.zeros((rows, 128), F32)
            for i in range(switches):
                w = jnp.where(lanes == i, weights[i], w)
            wown[c] = w

            @pl.when(jnp.logical_not(first))
            def _():
                w_copy(c).start()

            back(c)

    each(ahead)

    @pl.when(jnp.logical_not(last))
    def _():
        def later(c):
            w_copy(c).wait_recv()
            wown[c] = wrecv[c]

            @pl.when(jnp.logical_not(first))
            def _():
                w_copy(c).start()

            back(c)

        each(later)

    each(lambda c: x_copy(c, other).wait_recv())
    joined[0:bus] = xfull[...].reshape(topo, bus).T

    @pl.when(last)
    def _():
        joined[bus:2 * bus] = jnp.zeros((bus, topo), F32)

    @pl.when(jnp.logical_not(last))
    def _():
        def arrive(c):
            n_copy(c, 0, 0).wait_recv()
            n_copy(c, 1, 0).wait_recv()

        each(arrive)
        joined[bus:2 * bus] = xnext[...].reshape(topo, bus).T

        def sent(c):
            y_copy(c).wait_send()
            t_copy(c).wait_send()

        each(sent)

    @pl.when(jnp.logical_not(first))
    def _():
        def sent(c):
            w_copy(c).wait_send()
            c_copy(c).wait_send()
            n_copy(c, line, 0).wait_send()
            n_copy(c, line, 1).wait_send()

        each(sent)

    each(lambda c: x_copy(c, line).wait_send())


def pool_kernel(br_from, br_to, br_susc, br_owner, joined, weight, bias, acc, wide_w, wide_b, wide_t):
    hidden, topo = wide_w.shape
    wide_w[...] = jnp.broadcast_to(weight[...], (hidden, topo))
    wide_b[...] = jnp.broadcast_to(bias[...], (hidden, topo))
    wide_t[...] = jnp.tanh(wide_b[...])
    acc[...] = jnp.zeros_like(acc)
    step_rows = 32

    def group(g, carry):
        flows, owners = [], []
        for u in range(UNROLL):
            at = g * UNROLL + u
            difference = joined[pl.ds(br_from[at], 1), :] - joined[pl.ds(br_to[at], 1), :]
            flows.append(br_susc[at] * difference)
            owners.append(br_owner[at])
        for h in range(0, hidden, step_rows):
            part = pl.ds(h, step_rows)
            w, b, t = wide_w[part, :], wide_b[part, :], wide_t[part, :]
            values = [jnp.tanh(flow * w + b) - t for flow in flows]
            for owner, value in zip(owners, values):
                acc[owner, part, :] += value
        return carry

    lax.fori_loop(0, br_from.shape[0] // UNROLL, group, 0)


def share_kernel(fronts, acc, out_weight, scores, paired, summed, arrived, p_s, p_r, s_s, s_r):
    me, line = lax.axis_index("front"), lax.axis_index("line")
    other = 1 - line
    greet(me, other)

    def hello(step, carry):
        greet(lax.rem(me + step, fronts), line)
        return carry

    lax.fori_loop(1, fronts, hello, 0)
    pl.semaphore_wait(pltpu.get_barrier_semaphore(), fronts)

    def p_copy(f):
        return copy_to(acc.at[f * 2 + other], paired.at[f], p_s.at[f], p_r.at[f], me, other)

    def s_copy(f, origin, slot):
        return copy_to(summed.at[f], arrived.at[origin], s_s.at[f], s_r.at[slot], f, line)

    def turn(fn, own):
        def step(at, carry):
            fn(lax.rem(me + at, fronts))
            return carry

        lax.fori_loop(1, fronts + own, step, 0)

    turn(lambda f: p_copy(f).start(), 1)

    def pair(f):
        p_copy(f).wait_recv()
        summed[f] = acc[f * 2 + line] + paired[f]

        @pl.when(f != me)
        def _():
            s_copy(f, me, me).start()

    turn(pair, 1)
    turn(lambda f: s_copy(f, f, f).wait_recv(), 0)
    arrived[me] = summed[me]

    def add(f, total):
        return total + arrived[f]

    total = lax.fori_loop(1, fronts, add, arrived[0])
    pooled = (total * SCALE).T.astype(BF16)
    scores[...] = dot(pooled, out_weight[...]).astype(BF16)
    turn(lambda f: p_copy(f).wait_send(), 1)
    turn(lambda f: s_copy(f, me, me).wait_send(), 0)


def body(
    injections, switch_from, switch_to, switch_susc, coupling, pivot_inverse,
    branch_from, branch_to, branch_susc, branch_owner, in_weight, in_bias, out_weight,
):
    fronts = lax.axis_size("front")
    bus, topo = injections.shape
    switches = switch_from.shape[0]
    hidden = in_weight.shape[0]
    rows = topo // (2 * CHUNKS)
    many = (switches + 1) * rows
    owners = lax.axis_size(("front", "line"))
    vmem = pl.BlockSpec(memory_space=pltpu.VMEM)
    smem = pl.BlockSpec(memory_space=pltpu.SMEM)
    dma = pltpu.SemaphoreType.DMA
    full = lambda *shape: pltpu.VMEM(shape, F32)
    half = pltpu.VMEM((2, bus, bus), BF16)

    joined = pl.pallas_call(
        functools.partial(solve_kernel, fronts),
        out_shape=jax.ShapeDtypeStruct((2 * bus, topo), F32),
        in_specs=[vmem] * 6,
        out_specs=vmem,
        scratch_shapes=[
            full(CHUNKS, many, bus), full(CHUNKS, many, bus), full(CHUNKS, many, bus),
            full(CHUNKS, rows, 128), full(CHUNKS, rows, 128),
            full(CHUNKS, rows, 128), full(CHUNKS, rows, 128),
            full(CHUNKS, rows, bus), full(CHUNKS, rows, bus),
            full(2, CHUNKS, rows, bus), full(2, CHUNKS, rows, bus), full(2, CHUNKS, rows, bus),
            half, half, half,
        ] + [dma((CHUNKS,))] * 10 + [dma((2, CHUNKS))] * 2,
        compiler_params=pltpu.CompilerParams(
            collective_id=0, has_side_effects=True, vmem_limit_bytes=VMEM_BYTES
        ),
        name="solve",
    )(injections, switch_from.T, switch_to.T, switch_susc.T, coupling, pivot_inverse)

    first_bus = lax.axis_index("front") * bus
    acc = pl.pallas_call(
        pool_kernel,
        out_shape=jax.ShapeDtypeStruct((owners, hidden, topo), F32),
        in_specs=[smem] * 4 + [vmem] * 3,
        out_specs=vmem,
        scratch_shapes=[full(hidden, topo)] * 3,
        compiler_params=pltpu.CompilerParams(vmem_limit_bytes=VMEM_BYTES),
        name="pool",
    )(
        jnp.clip(branch_from - first_bus, 0, 2 * bus - 1),
        jnp.clip(branch_to - first_bus, 0, 2 * bus - 1),
        branch_susc,
        jnp.clip(branch_owner[:, 0], 0, owners - 1),
        joined,
        in_weight[:, None],
        in_bias[:, None],
    )

    scores = pl.pallas_call(
        functools.partial(share_kernel, fronts),
        out_shape=jax.ShapeDtypeStruct((topo, out_weight.shape[1]), BF16),
        in_specs=[vmem] * 2,
        out_specs=vmem,
        scratch_shapes=[full(fronts, hidden, topo)] * 3 + [dma((fronts,))] * 4,
        compiler_params=pltpu.CompilerParams(
            collective_id=1, has_side_effects=True, vmem_limit_bytes=VMEM_BYTES
        ),
        name="share",
    )(acc, out_weight)
    return (scores[None], joined[0:bus])


def solution(mesh):
    in_specs = (
        P("front", ("groups", "batch")),
        P(None, ("groups", "batch")),
        P(None, ("groups", "batch")),
        P(None, ("groups", "batch")),
        P("front", None),
        P("front", None),
        P(("front", "line")),
        P(("front", "line")),
        P(("front", "line")),
        P(("front", "line"), None),
        P(),
        P(),
        P(),
    )
    out_specs = (P(("front", "line"), ("groups", "batch"), None), P("front", ("groups", "batch")))
    return jax.shard_map(body, mesh=mesh, in_specs=in_specs, out_specs=out_specs, check_vma=False)
```

time: 244 us -> 74.3 us (0.30)
  waiting for transfers between devices: 118 us -> 0 us
  Pallas kernels: 0 us -> 62.7 us
  matrix products: 34.9 us -> 0 us
  other arithmetic: 32.3 us -> 0.01 us
  starting transfers between devices: 24.9 us -> 0 us
  blocking collectives: 19.6 us -> 0 us
    ppermute x7 -> x0, waiting for transfers between devices: 102 us -> none  [from_behind(): return lax.ppermute(value, axis, pairs)]
    pallas_call x0 -> x3, Pallas kernels: none -> 62.7 us  [the longest x1 39.8 us: body(): pl.pallas_call(functools.partial(solve_kernel, fronts), out_shape=jax.Sha...]
    dot_general x10 -> x0, matrix products: 34.9 us -> none  [the longest x8 29.7 us: product(): jnp.dot(operand, against, precision=lax.Precision.HIGHEST, preferred_elem...]
    reduce_sum x33 -> x0, other arithmetic: 23.1 us -> none  [the longest x32 23 us: accumulate(): jnp.sum(centered_tanh(slot_block, in_weight, in_bias), axis=0)]
    ppermute x7 -> x0, starting transfers between devices: 21.5 us -> none  [from_behind(): return lax.ppermute(value, axis, pairs)]
    psum x1 -> x0, blocking collectives: 19.6 us -> none  [body(): terms = lax.psum(local_terms, 'front')]
    all_to_all x1 -> x0, waiting for transfers between devices: 15.2 us -> none  [body(): lax.all_to_all(outgoing, ('front', 'line'), split_axis=0, concat_axis=0,...]
    sub x5 -> x0, other arithmetic: 7.19 us -> none  [the longest x3 6.31 us: upper_step(): return pivoted - arrived]
  transfers between devices with their start and end apart: 8 -> 0, of which waited for: 8 -> 0; matrix products, arithmetic and copies ran while one was open for 1% -> 0% of each run, Pallas kernels for 0% -> 0%
where the time goes in v1:
time: 74.3 us; the launch traced here: 73.9 us
  Pallas kernels  62.7 us (84%)
  local copies, waits for them, and re-layouts  10.6 us (14%)
    pallas_call x1, Pallas kernels, body(): pl.pallas_call(functools.partial(solve_kernel, fronts), out_shape=jax.Sha...  39.8 us
    pallas_call x1, Pallas kernels, body(): pl.pallas_call(pool_kernel, out_shape=jax.ShapeDtypeStruct((owners, hidde...  12.4 us
    pallas_call x1, Pallas kernels, body(): pl.pallas_call(functools.partial(share_kernel, fronts), out_shape=jax.Sha...  10.4 us
    unnamed x28, local copies, waits for them, and re-layouts  9.61 us

profile of v1, /device:TPU:0, one launch (start us, length us, event | category | flops | bytes accessed | tf_op | source)
XLA Modules:
  0.0 73.9 jit_solution(13851554722888809006)
XLA Ops:
  0.6 0.8 %copy.15 = s32[2,128]{0,1:T(8,128)S(1)} copy(s32[2,128]{1,0:T(2,128)} %param.14) | data formatting | bytes 2048 | tf_op args[1]
  1.4 0.0 copy-start.8
  1.4 0.7 copy-done.8
  2.1 0.1 copy.16
  2.2 0.0 copy-start.9
  2.2 0.7 copy-done.9
  2.9 0.1 copy.17
  3.0 0.0 copy-start
  3.0 1.2 %copy-done = f32[512,512]{1,0:T(8,128)S(1)} copy-done((f32[512,512]{1,0:T(8,128)S(1)}, f32[512,512]{1,0:T(8,128)}, u32[]{:S(2)}) %copy-start) | copy-done | bytes 1048600
  4.2 0.0 copy-start.1
  4.2 1.2 %copy-done.1 = f32[512,512]{1,0:T(8,128)S(1)} copy-done((f32[512,512]{1,0:T(8,128)S(1)}, f32[512,512]{1,0:T(8,128)}, u32[]{:S(2)}) %copy-start.1) | copy-done | bytes 1048600
  5.5 0.0 copy-start.2
  5.5 0.9 %copy-done.2 = f32[512,128]{1,0:T(8,128)S(1)} copy-done((f32[512,128]{1,0:T(8,128)S(1)}, f32[512,128]{1,0:T(8,128)}, u32[]{:S(2)}) %copy-start.2) | copy-done | bytes 262168
  6.4 39.8 %solve.1.joined = f32[1024,128]{1,0:T(8,128)S(1)} custom-call(f32[512,128]{1,0:T(8,128)S(1)} %copy-done.2, s32[128,2]{1,0:T(8,128)S(1)} %bitcast.7, s32[128,2]{1,0:T(8,128)S(1)} %bitcast.8, f32[128,2]{1,0:T(8,128)S(1)} %bitcast.9, f32[512,512]{1,0:T(8,128)S(1)} %copy-done, f32[512,512]{1,0:T(8,128)S(1)} %copy-done.1), custom_call_target="tpu_custom_call" | custom-call | tf_op jit(solution)/shard_map/solve/pallas_call | solution.py:378
  46.2 0.0 copy-start.6
  46.2 0.0 copy-start.5
  46.3 0.7 copy-done.6
  46.9 0.0 copy-done.5
  46.9 0.0 copy-start.10
  46.9 0.7 copy-done.10
  47.6 0.1 copy.18.weight
  47.7 0.0 copy-start.11
  47.7 0.7 copy-done.11
  48.4 0.0 copy-start.7
  48.4 0.1 copy.19.bias
  48.5 0.6 copy-done.7
  49.0 0.0 copy-start.4
  49.1 0.7 copy-done.4
  49.7 0.0 copy-start.3
  49.7 12.4 %pool.1.acc = f32[8,128,128]{2,1,0:T(8,128)S(1)} custom-call(s32[512]{0:T(512)S(1)} %get-tuple-element.3.br_from, s32[512]{0:T(512)S(1)} %get-tuple-element.2.br_to, f32[512]{0:T(512)S(1)} %copy-done.4, s32[512]{0:T(512)S(1)} %bitcast.11, f32[1024,128]{1,0:T(8,128)S(1)} %solve.1.joined, f32[128,1]{1,0:T(8,128)S(1)} %copy.18.weight, f32[128,1]{1,0:T(8,128)S(1)} %copy.19.bias), custom_call_target="tpu_custom_call" | custom-call | tf_op jit(solution)/shard_map/pool/pallas_call | solution.py:398
  62.2 0.0 copy-done.3
  62.2 10.4 %share.1 = bf16[128,128]{1,0:T(8,128)(2,1)S(1)} custom-call(f32[8,128,128]{2,1,0:T(8,128)S(1)} %pool.1.acc, bf16[128,128]{1,0:T(8,128)(2,1)S(1)} %copy-done.3), custom_call_target="tpu_custom_call" | custom-call | tf_op jit(solution)/shard_map/share/pallas_call | solution.py:416
  72.6 0.7 slice.3
  73.3 0.6 copy.21
  (2 shorter events, 0.0 us)
Async XLA Ops:
  1.4 0.7 copy-start.8
  2.2 0.7 copy-start.9
  3.0 1.2 %copy-start = (f32[512,512]{1,0:T(8,128)S(1)}, f32[512,512]{1,0:T(8,128)}, u32[]{:S(2)}) copy-start(f32[512,512]{1,0:T(8,128)} %coupling.1) | copy-start | bytes 3145732
  4.2 1.2 %copy-start.1 = (f32[512,512]{1,0:T(8,128)S(1)}, f32[512,512]{1,0:T(8,128)}, u32[]{:S(2)}) copy-start(f32[512,512]{1,0:T(8,128)} %pivot.1) | copy-start | bytes 3145732
  5.5 0.9 %copy-start.2 = (f32[512,128]{1,0:T(8,128)S(1)}, f32[512,128]{1,0:T(8,128)}, u32[]{:S(2)}) copy-start(f32[512,128]{1,0:T(8,128)} %inj.1) | copy-start | bytes 786436
  46.2 0.7 copy-start.6
  46.2 0.7 copy-start.5
  46.9 0.7 copy-start.10
  47.7 0.7 copy-start.11
  48.4 0.7 copy-start.7
  49.0 0.7 copy-start.4
  49.7 12.4 %copy-start.3 = (bf16[128,128]{1,0:T(8,128)(2,1)S(1)}, bf16[128,128]{1,0:T(8,128)(2,1)}, u32[]{:S(2)}) copy-start(bf16[128,128]{1,0:T(8,128)(2,1)} %out_weight.1) | copy-start | bytes 98308

commit v2 on v1

--- a/solution.py
+++ b/solution.py
@@ -9,6 +9,7 @@
 
 CHUNKS = 4
 UNROLL = 8
+WIDE = 16
 SCALE = 512 ** (-0.5)
 F32, BF16 = jnp.float32, jnp.bfloat16
 VMEM_BYTES = 40 * 1024 * 1024
@@ -25,7 +26,9 @@
 
 def product(operand, against):
     high, low = split(operand)
-    return dot(high, against[0]) + (dot(low, against[0]) + dot(high, against[1]))
+    rows = operand.shape[0]
+    both = dot(jnp.concatenate([high, low], axis=0), against[0])
+    return both[:rows] + (both[rows:] + dot(high, against[1]))
 
 
 def copy_to(src, dst, send_sem, recv_sem, front, line):
@@ -80,51 +83,78 @@
 def solve_kernel(
     fronts, inj, sw_from, sw_to, sw_susc, coupling, pivot, joined,
     yown, yrecv, zown, town, trecv, wown, wrecv, cown, crecv, xfull, xnext, injt,
-    e_fwd, e_back, p_fwd,
-    y_s, y_r, t_s, t_r, w_s, w_r, c_s, c_r, x_s, x_r, n_s, n_r,
+    e_fwd, e_back, p_fwd, sw_wide, to_wide, susc_wide,
+    inj_v, e_v, p_v,
+    y_s, y_r, t_s, t_r, w_s, w_r, c_s, c_r, x_s, x_r, n_s, n_r, r_s, r_r, load,
 ):
     me, line = lax.axis_index("front"), lax.axis_index("line")
     other = 1 - line
     first, last = me == 0, me == fronts - 1
     bus, topo = inj.shape
-    switches = sw_from.shape[1]
+    switches = sw_from.shape[0]
     rows = topo // (2 * CHUNKS)
     kinds = switches + 1
     pairs = [(i, c) for i in range(switches) for c in range(i + 2)]
 
+    inj_load = pltpu.make_async_copy(inj, inj_v, load.at[0])
+    e_load = pltpu.make_async_copy(coupling, e_v, load.at[1])
+    p_load = pltpu.make_async_copy(pivot, p_v, load.at[2])
+    inj_load.start()
+    e_load.start()
+    p_load.start()
     greet(me, other)
 
     @pl.when(jnp.logical_not(first))
     def _():
-        greet(me - 1, 0)
-        greet(me - 1, 1)
+        greet(me - 1, line)
 
     @pl.when(jnp.logical_not(last))
     def _():
-        greet(me + 1, 0)
-        greet(me + 1, 1)
-
-    injt[...] = inj[...].T.reshape(injt.shape)
+        greet(me + 1, line)
+
+    def wide(ref, kind):
+        fill = jnp.zeros((8 - switches, topo), kind)
+        return jnp.concatenate([ref[...], fill], axis=0).T
+
+    sw_wide[...] = wide(sw_from, jnp.int32)
+    to_wide[...] = wide(sw_to, jnp.int32)
+    susc_wide[...] = wide(sw_susc, F32)
+    inj_load.wait()
+    injt[...] = inj_v[...].T.reshape(injt.shape)
 
     def stack(c, carry):
         yown[c, 0:rows] = injt[line, c]
         ids = me * bus + lax.broadcasted_iota(jnp.int32, (rows, bus), 1)
         at = pl.ds(pl.multiple_of((line * CHUNKS + c) * rows, rows), rows)
-        f, t = sw_from[at, :], sw_to[at, :]
+        f, t = sw_wide[at, :], to_wide[at, :]
+
+        def incidence(i, ids):
+            return (ids == f[:, i:i + 1]).astype(F32) - (ids == t[:, i:i + 1]).astype(F32)
+
         for i in range(switches):
-            yown[c, (1 + i) * rows:(2 + i) * rows] = (ids == f[:, i:i + 1]).astype(F32) - (
-                ids == t[:, i:i + 1]
-            ).astype(F32)
+            part = slice((1 + i) * rows, (2 + i) * rows)
+            yown[c, part] = incidence(i, ids)
+
+            @pl.when(me == 1)
+            def _():
+                yrecv[c, part] = incidence(i, ids - bus)
+
         return carry
 
     lax.fori_loop(0, CHUNKS, stack, 0)
     pl.semaphore_wait(
         pltpu.get_barrier_semaphore(),
-        1 + 2 * jnp.where(first, 0, 1) + 2 * jnp.where(last, 0, 1),
+        1 + jnp.where(first, 0, 1) + jnp.where(last, 0, 1),
     )
 
     def y_copy(c):
         return copy_to(yown.at[c], yrecv.at[c], y_s.at[c], y_r.at[c], me + 1, line)
+
+    def first_copy(c):
+        part = pl.ds(0, rows)
+        return copy_to(
+            yown.at[c, part], yrecv.at[c, part], y_s.at[c], y_r.at[c], me + 1, line
+        )
 
     def t_copy(c):
         return copy_to(town.at[c], trecv.at[c], t_s.at[c], t_r.at[c], me + 1, line)
@@ -139,10 +169,18 @@
         place = xfull.at[half, c]
         return copy_to(place, place, x_s.at[c], x_r.at[c], me, other)
 
-    def n_copy(c, half, to):
+    def n_copy(c):
         return copy_to(
-            xfull.at[half, c], xnext.at[half, c], n_s.at[to, c], n_r.at[half, c], me - 1, to
+            xfull.at[line, c], xnext.at[line, c], n_s.at[c], n_r.at[c], me - 1, line
         )
+
+    def r_copy(c, half):
+        place = xnext.at[half, c]
+        return copy_to(place, place, r_s.at[c], r_r.at[c], me, other)
+
+    def relay(c):
+        n_copy(c).wait_recv()
+        r_copy(c, line).start()
 
     def each(fn):
         def step(c, carry):
@@ -153,11 +191,13 @@
 
     @pl.when(first)
     def _():
-        each(lambda c: y_copy(c).start())
-
-    e_fwd[0], e_fwd[1] = split(coupling[...].T)
-    p_fwd[0], p_fwd[1] = split(pivot[...].T)
-    e_back[0], e_back[1] = split(coupling[...])
+        each(lambda c: first_copy(c).start())
+
+    e_load.wait()
+    e_fwd[0], e_fwd[1] = split(e_v[...].T)
+    e_back[0], e_back[1] = split(e_v[...])
+    p_load.wait()
+    p_fwd[0], p_fwd[1] = split(p_v[...].T)
     lanes = lax.broadcasted_iota(jnp.int32, (rows, 128), 1)
 
     def back(c):
@@ -176,15 +216,21 @@
         def _():
             cown[c] = product(xfull[line, c], e_back)
             c_copy(c).start()
-            n_copy(c, line, 0).start()
-            n_copy(c, line, 1).start()
+            n_copy(c).start()
 
         x_copy(c, line).start()
 
     def ahead(c):
         @pl.when(jnp.logical_not(first))
         def _():
-            y_copy(c).wait_recv()
+            @pl.when(me == 1)
+            def _():
+                first_copy(c).wait_recv()
+
+            @pl.when(me > 1)
+            def _():
+                y_copy(c).wait_recv()
+
             yown[c] = yown[c] - product(yrecv[c], e_fwd)
 
             @pl.when(jnp.logical_not(last))
@@ -219,7 +265,7 @@
             for j, (i, k) in enumerate(pairs):
                 terms[i][k] = total[:, j:j + 1]
             at = pl.ds(pl.multiple_of((line * CHUNKS + c) * rows, rows), rows)
-            susc = sw_susc[at, :]
+            susc = susc_wide[at, :]
             weights = capacitance_solve(terms, [susc[:, i:i + 1] for i in range(switches)])
             w = jnp.zeros((rows, 128), F32)
             for i in range(switches):
@@ -246,7 +292,12 @@
 
             back(c)
 
+            @pl.when(c > 0)
+            def _():
+                relay(c - 1)
+
         each(later)
+        relay(CHUNKS - 1)
 
     each(lambda c: x_copy(c, other).wait_recv())
     joined[0:bus] = xfull[...].reshape(topo, bus).T
@@ -257,15 +308,19 @@
 
     @pl.when(jnp.logical_not(last))
     def _():
-        def arrive(c):
-            n_copy(c, 0, 0).wait_recv()
-            n_copy(c, 1, 0).wait_recv()
-
-        each(arrive)
+        each(lambda c: r_copy(c, other).wait_recv())
         joined[bus:2 * bus] = xnext[...].reshape(topo, bus).T
 
         def sent(c):
-            y_copy(c).wait_send()
+            @pl.when(first)
+            def _():
+                first_copy(c).wait_send()
+
+            @pl.when(jnp.logical_not(first))
+            def _():
+                y_copy(c).wait_send()
+
+            r_copy(c, line).wait_send()
             t_copy(c).wait_send()
 
         each(sent)
@@ -275,38 +330,67 @@
         def sent(c):
             w_copy(c).wait_send()
             c_copy(c).wait_send()
-            n_copy(c, line, 0).wait_send()
-            n_copy(c, line, 1).wait_send()
+            n_copy(c).wait_send()
 
         each(sent)
 
     each(lambda c: x_copy(c, line).wait_send())
 
 
-def pool_kernel(br_from, br_to, br_susc, br_owner, joined, weight, bias, acc, wide_w, wide_b, wide_t):
+def pool_kernel(
+    from_in, to_in, susc_in, owner_in, joined_in, weight, bias, acc, angles,
+    br_from, br_to, br_susc, joined, flows, wide_w, wide_b, wide_t, load,
+):
     hidden, topo = wide_w.shape
-    wide_w[...] = jnp.broadcast_to(weight[...], (hidden, topo))
-    wide_b[...] = jnp.broadcast_to(bias[...], (hidden, topo))
+    bus = joined.shape[0] // 2
+    first_bus = lax.axis_index("front") * bus
+    pairs = [
+        (from_in, br_from), (to_in, br_to), (susc_in, br_susc), (joined_in, joined),
+    ]
+    loads = [pltpu.make_async_copy(a, b, load.at[i]) for i, (a, b) in enumerate(pairs)]
+    for one in loads:
+        one.start()
+    wide_w[...] = jnp.broadcast_to(weight[...], (topo, hidden)).T
+    wide_b[...] = jnp.broadcast_to(bias[...], (topo, hidden)).T
     wide_t[...] = jnp.tanh(wide_b[...])
-    acc[...] = jnp.zeros_like(acc)
-    step_rows = 32
-
-    def group(g, carry):
-        flows, owners = [], []
+    owners, branches = acc.shape[0], flows.shape[0]
+    names = lax.broadcasted_iota(jnp.int32, (owners, branches), 0)
+    hot = (names == owner_in[...]).astype(F32).astype(BF16)
+    for one in loads:
+        one.wait()
+    store = pltpu.make_async_copy(joined.at[pl.ds(0, bus)], angles, load.at[4])
+    store.start()
+
+    def bus_row(bus_id):
+        at = jnp.minimum(jnp.maximum(bus_id - first_bus, 0), 2 * bus - 1)
+        return joined[pl.ds(at, 1), :]
+
+    def gather(g, carry):
         for u in range(UNROLL):
             at = g * UNROLL + u
-            difference = joined[pl.ds(br_from[at], 1), :] - joined[pl.ds(br_to[at], 1), :]
-            flows.append(br_susc[at] * difference)
-            owners.append(br_owner[at])
-        for h in range(0, hidden, step_rows):
-            part = pl.ds(h, step_rows)
-            w, b, t = wide_w[part, :], wide_b[part, :], wide_t[part, :]
-            values = [jnp.tanh(flow * w + b) - t for flow in flows]
-            for owner, value in zip(owners, values):
-                acc[owner, part, :] += value
+            row = bus_row(br_from[at]) - bus_row(br_to[at])
+            flows[pl.ds(at, 1), :] = br_susc[at] * row
         return carry
 
-    lax.fori_loop(0, br_from.shape[0] // UNROLL, group, 0)
+    lax.fori_loop(0, branches // UNROLL, gather, 0)
+
+    def pool(g, carry):
+        parts = []
+        for u in range(WIDE):
+            at = pl.ds(g * WIDE + u, 1)
+            shifted = jnp.tanh(flows[...] * wide_w[at, :] + wide_b[at, :])
+            parts.append((shifted - wide_t[at, :]).astype(BF16))
+        for u in range(0, WIDE, 2):
+            out = dot(hot, jnp.concatenate(parts[u:u + 2], axis=1))
+            for v in range(2):
+                for owner in range(owners):
+                    acc[owner, pl.ds(g * WIDE + u + v, 1), :] = out[
+                        owner:owner + 1, v * topo:(v + 1) * topo
+                    ]
+        return carry
+
+    lax.fori_loop(0, hidden // WIDE, pool, 0)
+    store.wait()
 
 
 def share_kernel(fronts, acc, out_weight, scores, paired, summed, arrived, p_s, p_r, s_s, s_r):
@@ -370,6 +454,7 @@
     many = (switches + 1) * rows
     owners = lax.axis_size(("front", "line"))
     vmem = pl.BlockSpec(memory_space=pltpu.VMEM)
+    hbm = pl.BlockSpec(memory_space=pl.ANY)
     smem = pl.BlockSpec(memory_space=pltpu.SMEM)
     dma = pltpu.SemaphoreType.DMA
     full = lambda *shape: pltpu.VMEM(shape, F32)
@@ -378,7 +463,7 @@
     joined = pl.pallas_call(
         functools.partial(solve_kernel, fronts),
         out_shape=jax.ShapeDtypeStruct((2 * bus, topo), F32),
-        in_specs=[vmem] * 6,
+        in_specs=[hbm] + [vmem] * 3 + [hbm] * 2,
         out_specs=vmem,
         scratch_shapes=[
             full(CHUNKS, many, bus), full(CHUNKS, many, bus), full(CHUNKS, many, bus),
@@ -387,30 +472,33 @@
             full(CHUNKS, rows, bus), full(CHUNKS, rows, bus),
             full(2, CHUNKS, rows, bus), full(2, CHUNKS, rows, bus), full(2, CHUNKS, rows, bus),
             half, half, half,
-        ] + [dma((CHUNKS,))] * 10 + [dma((2, CHUNKS))] * 2,
+            pltpu.VMEM((topo, 8), jnp.int32), pltpu.VMEM((topo, 8), jnp.int32), full(topo, 8),
+            full(bus, topo), full(bus, bus), full(bus, bus),
+        ] + [dma((CHUNKS,))] * 14 + [dma((3,))],
         compiler_params=pltpu.CompilerParams(
             collective_id=0, has_side_effects=True, vmem_limit_bytes=VMEM_BYTES
         ),
         name="solve",
-    )(injections, switch_from.T, switch_to.T, switch_susc.T, coupling, pivot_inverse)
-
-    first_bus = lax.axis_index("front") * bus
-    acc = pl.pallas_call(
+    )(injections, switch_from, switch_to, switch_susc, coupling, pivot_inverse)
+
+    branches = branch_from.shape[0]
+    acc, angles = pl.pallas_call(
         pool_kernel,
-        out_shape=jax.ShapeDtypeStruct((owners, hidden, topo), F32),
-        in_specs=[smem] * 4 + [vmem] * 3,
-        out_specs=vmem,
-        scratch_shapes=[full(hidden, topo)] * 3,
+        out_shape=(
+            jax.ShapeDtypeStruct((owners, hidden, topo), F32),
+            jax.ShapeDtypeStruct((bus, topo), F32),
+        ),
+        in_specs=[hbm] * 3 + [vmem] + [hbm] + [vmem] * 2,
+        out_specs=(vmem, hbm),
+        scratch_shapes=[
+            pltpu.SMEM((branches,), jnp.int32), pltpu.SMEM((branches,), jnp.int32),
+            pltpu.SMEM((branches,), F32), full(2 * bus, topo), full(branches, topo),
+        ] + [full(hidden, topo)] * 3 + [dma((5,))],
         compiler_params=pltpu.CompilerParams(vmem_limit_bytes=VMEM_BYTES),
         name="pool",
     )(
-        jnp.clip(branch_from - first_bus, 0, 2 * bus - 1),
-        jnp.clip(branch_to - first_bus, 0, 2 * bus - 1),
-        branch_susc,
-        jnp.clip(branch_owner[:, 0], 0, owners - 1),
-        joined,
-        in_weight[:, None],
-        in_bias[:, None],
+        branch_from, branch_to, branch_susc, branch_owner.T, joined,
+        in_weight[None], in_bias[None],
     )
 
     scores = pl.pallas_call(
@@ -424,7 +512,7 @@
         ),
         name="share",
     )(acc, out_weight)
-    return (scores[None], joined[0:bus])
+    return (scores[None], angles)
 
 
 def solution(mesh):

time: 74.3 us -> 59.1 us (0.80)
  Pallas kernels: 62.7 us -> 53.3 us
  local copies, waits for them, and re-layouts: 10.6 us -> 4.73 us
    pallas_call x1, Pallas kernels: 39.8 us -> 33.9 us  [body(): pl.pallas_call(functools.partial(solve_kernel, fronts), out_shape=jax.Sha...]
    unnamed x28 -> x27, local copies, waits for them, and re-layouts: 9.61 us -> 4.73 us
    pallas_call x1, Pallas kernels: 12.4 us -> 9.21 us  [body(): pl.pallas_call(pool_kernel, out_shape=(jax.ShapeDtypeStruct((owners, hidd...]
where the time goes in v2:
time: 59.1 us; the launch traced here: 58.8 us
  Pallas kernels  53.3 us (90%)
  local copies, waits for them, and re-layouts  4.73 us (8%)
  between operations  0.77 us (1%)
    pallas_call x1, Pallas kernels, body(): pl.pallas_call(functools.partial(solve_kernel, fronts), out_shape=jax.Sha...  33.9 us
    pallas_call x1, Pallas kernels, body(): pl.pallas_call(functools.partial(share_kernel, fronts), out_shape=jax.Sha...  10.2 us
    pallas_call x1, Pallas kernels, body(): pl.pallas_call(pool_kernel, out_shape=(jax.ShapeDtypeStruct((owners, hidd...  9.21 us
    unnamed x27, local copies, waits for them, and re-layouts  4.73 us

profile of v2, /device:TPU:0, one launch (start us, length us, event | category | flops | bytes accessed | tf_op | source)
XLA Modules:
  0.0 58.8 jit_solution(5486260460116695550)
XLA Ops:
  0.6 0.0 copy-start.9
  0.6 0.0 copy-start.10
  0.7 0.0 copy-start.8
  0.7 0.7 %copy-done.9 = s32[2,128]{1,0:T(2,128)S(1)} copy-done((s32[2,128]{1,0:T(2,128)S(1)}, s32[2,128]{1,0:T(2,128)}, u32[]{:S(2)}) %copy-start.9) | copy-done | bytes 1048
  1.3 0.0 copy-done.10
  1.3 0.0 copy-done.8
  1.3 0.0 copy-start
  1.3 1.2 %copy-done = f32[512,512]{1,0:T(8,128)S(1)} copy-done((f32[512,512]{1,0:T(8,128)S(1)}, f32[512,512]{1,0:T(8,128)}, u32[]{:S(2)}) %copy-start) | copy-done | bytes 1048600
  2.6 0.0 copy-start.1
  2.6 1.2 %copy-done.1 = f32[512,512]{1,0:T(8,128)S(1)} copy-done((f32[512,512]{1,0:T(8,128)S(1)}, f32[512,512]{1,0:T(8,128)}, u32[]{:S(2)}) %copy-start.1) | copy-done | bytes 1048600
  3.8 0.0 copy-start.2
  3.8 0.9 %copy-done.2 = f32[512,128]{1,0:T(8,128)S(1)} copy-done((f32[512,128]{1,0:T(8,128)S(1)}, f32[512,128]{1,0:T(8,128)}, u32[]{:S(2)}) %copy-start.2) | copy-done | bytes 262168
  4.7 0.0 copy-start.4
  4.7 0.0 copy-start.5
  4.8 0.0 copy-start.6
  4.8 0.0 copy-start.7
  4.8 0.0 copy-start.11
  4.8 0.0 copy-start.12
  4.8 33.9 %solve.1.joined_in = f32[1024,128]{1,0:T(8,128)S(1)} custom-call(f32[512,128]{1,0:T(8,128)S(1)} %copy-done.2, s32[2,128]{1,0:T(2,128)S(1)} %copy-done.8, s32[2,128]{1,0:T(2,128)S(1)} %copy-done.9, f32[2,128]{1,0:T(2,128)S(1)} %copy-done.10, f32[512,512]{1,0:T(8,128)S(1)} %copy-done, f32[512,512]{1,0:T(8,128)S(1)} %copy-done.1), custom_call_target="tpu_custom_call" | custom-call | tf_op jit(solution)/shard_map/solve/pallas_call | solution.py:463
  38.7 0.0 copy-done.4
  38.7 0.0 copy-done.5
  38.7 0.0 copy-done.6
  38.7 0.0 copy-done.7
  38.7 0.0 copy-done.11
  38.7 0.0 copy-done.12
  38.7 0.0 copy-start.3
  38.7 9.2 %pool.1 = (f32[8,128,128]{2,1,0:T(8,128)S(1)}, f32[512,128]{1,0:T(8,128)}) custom-call(s32[512]{0:T(512)S(1)} %copy-done.4, s32[512]{0:T(512)S(1)} %copy-done.5, f32[512]{0:T(512)S(1)} %copy-done.6, s32[1,512]{1,0:T(1,128)S(1)} %bitcast.5, f32[1024,128]{1,0:T(8,128)S(1)} %solve.1.joined_in, f32[1,128]{1,0:T(1,128)S(1)} %bitcast.6, f32[1,128]{1,0:T(1,128)S(1)} %bitcast.7), custom_call_target="tpu_custom_call" | custom-call | tf_op jit(solution)/shard_map/pool/pallas_call | solution.py:485
  48.0 0.0 copy-done.3
  48.0 10.2 %share.1 = bf16[128,128]{1,0:T(8,128)(2,1)S(1)} custom-call(f32[8,128,128]{2,1,0:T(8,128)S(1)} %get-tuple-element.4.acc, bf16[128,128]{1,0:T(8,128)(2,1)S(1)} %copy-done.3), custom_call_target="tpu_custom_call" | custom-call | tf_op jit(solution)/shard_map/share/pallas_call | solution.py:504
  58.2 0.6 %copy.16 = bf16[1,128,128]{2,1,0:T(8,128)(2,1)} copy(bf16[1,128,128]{2,1,0:T(8,128)(2,1)S(1)} %bitcast.4) | data formatting | bytes 65536
Async XLA Ops:
  0.6 0.7 %copy-start.9 = (s32[2,128]{1,0:T(2,128)S(1)}, s32[2,128]{1,0:T(2,128)}, u32[]{:S(2)}) copy-start(s32[2,128]{1,0:T(2,128)} %sw_to.1) | copy-start | bytes 3076
  0.6 0.7 %copy-start.10 = (f32[2,128]{1,0:T(2,128)S(1)}, f32[2,128]{1,0:T(2,128)}, u32[]{:S(2)}) copy-start(f32[2,128]{1,0:T(2,128)} %sw_susc.1) | copy-start | bytes 3076
  0.7 0.7 %copy-start.8 = (s32[2,128]{1,0:T(2,128)S(1)}, s32[2,128]{1,0:T(2,128)}, u32[]{:S(2)}) copy-start(s32[2,128]{1,0:T(2,128)} %sw_from.1) | copy-start | bytes 3076
  1.3 1.2 %copy-start = (f32[512,512]{1,0:T(8,128)S(1)}, f32[512,512]{1,0:T(8,128)}, u32[]{:S(2)}) copy-start(f32[512,512]{1,0:T(8,128)} %coupling.1) | copy-start | bytes 3145732
  2.6 1.2 %copy-start.1 = (f32[512,512]{1,0:T(8,128)S(1)}, f32[512,512]{1,0:T(8,128)}, u32[]{:S(2)}) copy-start(f32[512,512]{1,0:T(8,128)} %pivot.1) | copy-start | bytes 3145732
  3.8 0.9 %copy-start.2 = (f32[512,128]{1,0:T(8,128)S(1)}, f32[512,128]{1,0:T(8,128)}, u32[]{:S(2)}) copy-start(f32[512,128]{1,0:T(8,128)} %inj.1) | copy-start | bytes 786436
  4.7 33.9 %copy-start.4 = (s32[512]{0:T(512)S(1)}, s32[512]{0:T(512)}, u32[]{:S(2)}) copy-start(s32[512]{0:T(512)} %from_in.1) | copy-start | bytes 6148
  4.7 33.9 %copy-start.5 = (s32[512]{0:T(512)S(1)}, s32[512]{0:T(512)}, u32[]{:S(2)}) copy-start(s32[512]{0:T(512)} %to_in.1) | copy-start | bytes 6148
  4.8 33.9 %copy-start.6 = (f32[512]{0:T(512)S(1)}, f32[512]{0:T(512)}, u32[]{:S(2)}) copy-start(f32[512]{0:T(512)} %susc_in.1) | copy-start | bytes 6148
  4.8 34.0 %copy-start.7 = (s32[512,1]{0,1:T(1,128)S(1)}, s32[512,1]{0,1:T(1,128)}, u32[]{:S(2)}) copy-start(s32[512,1]{0,1:T(1,128)} %param.22) | copy-start | bytes 6148
  4.8 34.0 %copy-start.11 = (f32[128]{0:T(128)S(1)}, f32[128]{0:T(128)}, u32[]{:S(2)}) copy-start(f32[128]{0:T(128)} %param.23) | copy-start | bytes 1540
  4.8 34.0 %copy-start.12 = (f32[128]{0:T(128)S(1)}, f32[128]{0:T(128)}, u32[]{:S(2)}) copy-start(f32[128]{0:T(128)} %param.24) | copy-start | bytes 1540
  38.7 9.2 %copy-start.3 = (bf16[128,128]{1,0:T(8,128)(2,1)S(1)}, bf16[128,128]{1,0:T(8,128)(2,1)}, u32[]{:S(2)}) copy-start(bf16[128,128]{1,0:T(8,128)(2,1)} %out_weight.1) | copy-start | bytes 98308

commit v3 on v2

--- a/solution.py
+++ b/solution.py
@@ -10,6 +10,7 @@
 CHUNKS = 4
 UNROLL = 8
 WIDE = 16
+PARTS = 4
 SCALE = 512 ** (-0.5)
 F32, BF16 = jnp.float32, jnp.bfloat16
 VMEM_BYTES = 40 * 1024 * 1024
@@ -338,9 +339,23 @@
 
 
 def pool_kernel(
-    from_in, to_in, susc_in, owner_in, joined_in, weight, bias, acc, angles,
-    br_from, br_to, br_susc, joined, flows, wide_w, wide_b, wide_t, load,
+    fronts, from_in, to_in, susc_in, owner_in, joined_in, weight, bias, out_weight,
+    scores, angles,
+    br_from, br_to, br_susc, joined, flows, wide_w, wide_b, wide_t,
+    acc, paired, summed, arrived, load, p_s, p_r, s_s, s_r,
 ):
+    me, line = lax.axis_index("front"), lax.axis_index("line")
+    other = 1 - line
+    greet(me, other)
+
+    def loop(start, stop, fn):
+        def step(at, carry):
+            fn(at)
+            return carry
+
+        lax.fori_loop(start, stop, step, 0)
+
+    loop(1, fronts, lambda step: greet(lax.rem(me + step, fronts), line))
     hidden, topo = wide_w.shape
     bus = joined.shape[0] // 2
     first_bus = lax.axis_index("front") * bus
@@ -389,57 +404,76 @@
                     ]
         return carry
 
-    lax.fori_loop(0, hidden // WIDE, pool, 0)
-    store.wait()
-
-
-def share_kernel(fronts, acc, out_weight, scores, paired, summed, arrived, p_s, p_r, s_s, s_r):
-    me, line = lax.axis_index("front"), lax.axis_index("line")
-    other = 1 - line
-    greet(me, other)
-
-    def hello(step, carry):
-        greet(lax.rem(me + step, fronts), line)
-        return carry
-
-    lax.fori_loop(1, fronts, hello, 0)
-    pl.semaphore_wait(pltpu.get_barrier_semaphore(), fronts)
-
-    def p_copy(f):
-        return copy_to(acc.at[f * 2 + other], paired.at[f], p_s.at[f], p_r.at[f], me, other)
-
-    def s_copy(f, origin, slot):
-        return copy_to(summed.at[f], arrived.at[origin], s_s.at[f], s_r.at[slot], f, line)
-
-    def turn(fn, own):
-        def step(at, carry):
-            fn(lax.rem(me + at, fronts))
-            return carry
-
-        lax.fori_loop(1, fronts + own, step, 0)
-
-    turn(lambda f: p_copy(f).start(), 1)
-
-    def pair(f):
-        p_copy(f).wait_recv()
-        summed[f] = acc[f * 2 + line] + paired[f]
-
-        @pl.when(f != me)
-        def _():
-            s_copy(f, me, me).start()
-
-    turn(pair, 1)
-    turn(lambda f: s_copy(f, f, f).wait_recv(), 0)
+    span = hidden // PARTS
+
+    def part(q):
+        return pl.ds(pl.multiple_of(q * span, span), span)
+
+    def p_copy(q, f):
+        return copy_to(
+            acc.at[f * 2 + other, part(q)], paired.at[f, part(q)],
+            p_s.at[q, f], p_r.at[q, f], me, other,
+        )
+
+    def s_copy(q, f, origin):
+        return copy_to(
+            summed.at[f, part(q)], arrived.at[origin, part(q)],
+            s_s.at[q, f], s_r.at[q, origin], f, line,
+        )
+
+    def turned(at):
+        return lax.rem(me + at, fronts)
+
+    def work(q):
+        lax.fori_loop(q * (span // WIDE), (q + 1) * (span // WIDE), pool, 0)
+
+        @pl.when(q == 0)
+        def _():
+            pl.semaphore_wait(pltpu.get_barrier_semaphore(), fronts)
+
+        loop(1, fronts + 1, lambda at: p_copy(q, turned(at)).start())
+
+    def send_on(q):
+        def one(at):
+            f = turned(at)
+            p_copy(q, f).wait_recv()
+            summed[f, part(q)] = acc[f * 2 + line, part(q)] + paired[f, part(q)]
+
+            @pl.when(f != me)
+            def _():
+                s_copy(q, f, me).start()
+
+        loop(1, fronts + 1, one)
+
+    def stage(q):
+        work(q)
+
+        @pl.when(q > 0)
+        def _():
+            send_on(q - 1)
+
+    loop(0, PARTS, stage)
+    send_on(PARTS - 1)
     arrived[me] = summed[me]
 
-    def add(f, total):
-        return total + arrived[f]
-
-    total = lax.fori_loop(1, fronts, add, arrived[0])
+    def finish(q):
+        def one(at):
+            f = turned(at)
+            s_copy(q, f, f).wait_recv()
+
+        loop(1, fronts, one)
+
+    loop(0, PARTS, finish)
+    total = lax.fori_loop(1, fronts, lambda f, total: total + arrived[f], arrived[0])
     pooled = (total * SCALE).T.astype(BF16)
     scores[...] = dot(pooled, out_weight[...]).astype(BF16)
-    turn(lambda f: p_copy(f).wait_send(), 1)
-    turn(lambda f: s_copy(f, me, me).wait_send(), 0)
+
+    def close(q):
+        loop(1, fronts + 1, lambda at: p_copy(q, turned(at)).wait_send())
+        loop(1, fronts, lambda at: s_copy(q, turned(at), me).wait_send())
+
+    loop(0, PARTS, close)
+    store.wait()
 
 
 def body(
@@ -454,7 +488,7 @@
     many = (switches + 1) * rows
     owners = lax.axis_size(("front", "line"))
     vmem = pl.BlockSpec(memory_space=pltpu.VMEM)
-    hbm = pl.BlockSpec(memory_space=pl.ANY)
+    hbm = pl.BlockSpec(memory_space=pltpu.HBM)
     smem = pl.BlockSpec(memory_space=pltpu.SMEM)
     dma = pltpu.SemaphoreType.DMA
     full = lambda *shape: pltpu.VMEM(shape, F32)
@@ -482,36 +516,27 @@
     )(injections, switch_from, switch_to, switch_susc, coupling, pivot_inverse)
 
     branches = branch_from.shape[0]
-    acc, angles = pl.pallas_call(
-        pool_kernel,
+    scores, angles = pl.pallas_call(
+        functools.partial(pool_kernel, fronts),
         out_shape=(
-            jax.ShapeDtypeStruct((owners, hidden, topo), F32),
+            jax.ShapeDtypeStruct((topo, out_weight.shape[1]), BF16),
             jax.ShapeDtypeStruct((bus, topo), F32),
         ),
-        in_specs=[hbm] * 3 + [vmem] + [hbm] + [vmem] * 2,
+        in_specs=[hbm] * 3 + [vmem] + [hbm] + [vmem] * 3,
         out_specs=(vmem, hbm),
         scratch_shapes=[
             pltpu.SMEM((branches,), jnp.int32), pltpu.SMEM((branches,), jnp.int32),
             pltpu.SMEM((branches,), F32), full(2 * bus, topo), full(branches, topo),
-        ] + [full(hidden, topo)] * 3 + [dma((5,))],
-        compiler_params=pltpu.CompilerParams(vmem_limit_bytes=VMEM_BYTES),
+        ] + [full(hidden, topo)] * 3 + [full(owners, hidden, topo)]
+        + [full(fronts, hidden, topo)] * 3 + [dma((5,))] + [dma((PARTS, fronts))] * 4,
+        compiler_params=pltpu.CompilerParams(
+            collective_id=1, has_side_effects=True, vmem_limit_bytes=VMEM_BYTES
+        ),
         name="pool",
     )(
         branch_from, branch_to, branch_susc, branch_owner.T, joined,
-        in_weight[None], in_bias[None],
+        in_weight[None], in_bias[None], out_weight,
     )
-
-    scores = pl.pallas_call(
-        functools.partial(share_kernel, fronts),
-        out_shape=jax.ShapeDtypeStruct((topo, out_weight.shape[1]), BF16),
-        in_specs=[vmem] * 2,
-        out_specs=vmem,
-        scratch_shapes=[full(fronts, hidden, topo)] * 3 + [dma((fronts,))] * 4,
-        compiler_params=pltpu.CompilerParams(
-            collective_id=1, has_side_effects=True, vmem_limit_bytes=VMEM_BYTES
-        ),
-        name="share",
-    )(acc, out_weight)
     return (scores[None], angles)
 
 

time: 59.1 us -> 53.5 us (0.905)
  Pallas kernels: 53.3 us -> 47.1 us
  local copies, waits for them, and re-layouts: 4.73 us -> 5.43 us
    pallas_call x2 -> x1, Pallas kernels: 19.4 us -> 13.2 us  [body(): pl.pallas_call(functools.partial(pool_kernel, fronts), out_shape=(jax.Sha...]
    unnamed x27 -> x28, local copies, waits for them, and re-layouts: 4.73 us -> 5.43 us
where the time goes in v3:
time: 53.5 us; the launch traced here: 53.3 us
  Pallas kernels  47.1 us (88%)
  local copies, waits for them, and re-layouts  5.43 us (10%)
  between operations  0.76 us (1%)
    pallas_call x1, Pallas kernels, body(): pl.pallas_call(functools.partial(solve_kernel, fronts), out_shape=jax.Sha...  33.9 us
    pallas_call x1, Pallas kernels, body(): pl.pallas_call(functools.partial(pool_kernel, fronts), out_shape=(jax.Sha...  13.2 us
    unnamed x28, local copies, waits for them, and re-layouts  5.43 us

profile of v3, /device:TPU:0, one launch (start us, length us, event | category | flops | bytes accessed | tf_op | source)
XLA Modules:
  0.0 53.3 jit_solution(1430690511733360047)
XLA Ops:
  0.6 0.0 copy-start.9
  0.6 0.0 copy-start.10
  0.7 0.0 copy-start.8
  0.7 0.7 %copy-done.9 = s32[2,128]{1,0:T(2,128)S(1)} copy-done((s32[2,128]{1,0:T(2,128)S(1)}, s32[2,128]{1,0:T(2,128)}, u32[]{:S(2)}) %copy-start.9) | copy-done | bytes 1048
  1.3 0.0 copy-done.10
  1.3 0.0 copy-done.8
  1.3 0.0 copy-start
  1.3 1.2 %copy-done = f32[512,512]{1,0:T(8,128)S(1)} copy-done((f32[512,512]{1,0:T(8,128)S(1)}, f32[512,512]{1,0:T(8,128)}, u32[]{:S(2)}) %copy-start) | copy-done | bytes 1048600
  2.6 0.0 copy-start.1
  2.6 1.2 %copy-done.1 = f32[512,512]{1,0:T(8,128)S(1)} copy-done((f32[512,512]{1,0:T(8,128)S(1)}, f32[512,512]{1,0:T(8,128)}, u32[]{:S(2)}) %copy-start.1) | copy-done | bytes 1048600
  3.8 0.0 copy-start.2
  3.8 0.9 %copy-done.2 = f32[512,128]{1,0:T(8,128)S(1)} copy-done((f32[512,128]{1,0:T(8,128)S(1)}, f32[512,128]{1,0:T(8,128)}, u32[]{:S(2)}) %copy-start.2) | copy-done | bytes 262168
  4.7 0.0 copy-start.3
  4.8 0.0 copy-start.4
  4.8 0.0 copy-start.5
  4.8 0.0 copy-start.6
  4.8 0.0 copy-start.7
  4.8 0.0 copy-start.11
  4.8 0.0 copy-start.12
  4.8 33.9 %solve.1.joined_in = f32[1024,128]{1,0:T(8,128)S(1)} custom-call(f32[512,128]{1,0:T(8,128)S(1)} %copy-done.2, s32[2,128]{1,0:T(2,128)S(1)} %copy-done.8, s32[2,128]{1,0:T(2,128)S(1)} %copy-done.9, f32[2,128]{1,0:T(2,128)S(1)} %copy-done.10, f32[512,512]{1,0:T(8,128)S(1)} %copy-done, f32[512,512]{1,0:T(8,128)S(1)} %copy-done.1), custom_call_target="tpu_custom_call" | custom-call | tf_op jit(solution)/shard_map/solve/pallas_call | solution.py:497
  38.7 0.0 copy-done.3
  38.7 0.0 copy-done.4
  38.7 0.0 copy-done.5
  38.7 0.0 copy-done.6
  38.7 0.0 copy-done.7
  38.7 0.0 copy-done.11
  38.7 0.0 copy-done.12
  38.7 13.2 %pool.1 = (bf16[128,128]{1,0:T(8,128)(2,1)S(1)}, f32[512,128]{1,0:T(8,128)S(1)}) custom-call(s32[512]{0:T(512)S(1)} %copy-done.4, s32[512]{0:T(512)S(1)} %copy-done.5, f32[512]{0:T(512)S(1)} %copy-done.6, s32[1,512]{1,0:T(1,128)S(1)} %bitcast.5, f32[1024,128]{1,0:T(8,128)S(1)} %solve.1.joined_in, f32[1,128]{1,0:T(1,128)S(1)} %bitcast.6, ...), custom_call_target="tpu_custom_call" | custom-call | tf_op jit(solution)/shard_map/pool/pallas_call | solution.py:519
  51.9 0.6 %copy.17 = bf16[1,128,128]{2,1,0:T(8,128)(2,1)} copy(bf16[1,128,128]{2,1,0:T(8,128)(2,1)S(1)} %bitcast.4) | data formatting | bytes 65536
  52.5 0.7 %copy.18 = f32[512,128]{1,0:T(8,128)} copy(f32[512,128]{1,0:T(8,128)S(1)} %get-tuple-element.9) | data formatting | bytes 524288
Async XLA Ops:
  0.6 0.7 %copy-start.9 = (s32[2,128]{1,0:T(2,128)S(1)}, s32[2,128]{1,0:T(2,128)}, u32[]{:S(2)}) copy-start(s32[2,128]{1,0:T(2,128)} %sw_to.1) | copy-start | bytes 3076
  0.6 0.7 %copy-start.10 = (f32[2,128]{1,0:T(2,128)S(1)}, f32[2,128]{1,0:T(2,128)}, u32[]{:S(2)}) copy-start(f32[2,128]{1,0:T(2,128)} %sw_susc.1) | copy-start | bytes 3076
  0.7 0.7 %copy-start.8 = (s32[2,128]{1,0:T(2,128)S(1)}, s32[2,128]{1,0:T(2,128)}, u32[]{:S(2)}) copy-start(s32[2,128]{1,0:T(2,128)} %sw_from.1) | copy-start | bytes 3076
  1.3 1.2 %copy-start = (f32[512,512]{1,0:T(8,128)S(1)}, f32[512,512]{1,0:T(8,128)}, u32[]{:S(2)}) copy-start(f32[512,512]{1,0:T(8,128)} %coupling.1) | copy-start | bytes 3145732
  2.6 1.2 %copy-start.1 = (f32[512,512]{1,0:T(8,128)S(1)}, f32[512,512]{1,0:T(8,128)}, u32[]{:S(2)}) copy-start(f32[512,512]{1,0:T(8,128)} %pivot.1) | copy-start | bytes 3145732
  3.8 0.9 %copy-start.2 = (f32[512,128]{1,0:T(8,128)S(1)}, f32[512,128]{1,0:T(8,128)}, u32[]{:S(2)}) copy-start(f32[512,128]{1,0:T(8,128)} %inj.1) | copy-start | bytes 786436
  4.7 33.9 %copy-start.3 = (bf16[128,128]{1,0:T(8,128)(2,1)S(1)}, bf16[128,128]{1,0:T(8,128)(2,1)}, u32[]{:S(2)}) copy-start(bf16[128,128]{1,0:T(8,128)(2,1)} %out_weight.1) | copy-start | bytes 98308
  4.8 33.9 %copy-start.4 = (s32[512]{0:T(512)S(1)}, s32[512]{0:T(512)}, u32[]{:S(2)}) copy-start(s32[512]{0:T(512)} %from_in.1) | copy-start | bytes 6148
  4.8 33.9 %copy-start.5 = (s32[512]{0:T(512)S(1)}, s32[512]{0:T(512)}, u32[]{:S(2)}) copy-start(s32[512]{0:T(512)} %to_in.1) | copy-start | bytes 6148
  4.8 34.0 %copy-start.6 = (f32[512]{0:T(512)S(1)}, f32[512]{0:T(512)}, u32[]{:S(2)}) copy-start(f32[512]{0:T(512)} %susc_in.1) | copy-start | bytes 6148
  4.8 34.0 %copy-start.7 = (s32[512,1]{0,1:T(1,128)S(1)}, s32[512,1]{0,1:T(1,128)}, u32[]{:S(2)}) copy-start(s32[512,1]{0,1:T(1,128)} %param.22) | copy-start | bytes 6148
  4.8 34.0 %copy-start.11 = (f32[128]{0:T(128)S(1)}, f32[128]{0:T(128)}, u32[]{:S(2)}) copy-start(f32[128]{0:T(128)} %param.23) | copy-start | bytes 1540
  4.8 34.0 %copy-start.12 = (f32[128]{0:T(128)S(1)}, f32[128]{0:T(128)}, u32[]{:S(2)}) copy-start(f32[128]{0:T(128)} %param.24) | copy-start | bytes 1540

commit v4 on v3

--- a/solution.py
+++ b/solution.py
@@ -8,12 +8,13 @@
 from jax.sharding import PartitionSpec as P
 
 CHUNKS = 4
-UNROLL = 8
+UNROLL = 32
 WIDE = 16
 PARTS = 4
 SCALE = 512 ** (-0.5)
 F32, BF16 = jnp.float32, jnp.bfloat16
 VMEM_BYTES = 40 * 1024 * 1024
+SOLVE_BYTES = 60 * 1024 * 1024
 
 
 def split(value):
@@ -510,7 +511,7 @@
             full(bus, topo), full(bus, bus), full(bus, bus),
         ] + [dma((CHUNKS,))] * 14 + [dma((3,))],
         compiler_params=pltpu.CompilerParams(
-            collective_id=0, has_side_effects=True, vmem_limit_bytes=VMEM_BYTES
+            collective_id=0, has_side_effects=True, vmem_limit_bytes=SOLVE_BYTES
         ),
         name="solve",
     )(injections, switch_from, switch_to, switch_susc, coupling, pivot_inverse)

time: 53.5 us -> 51.9 us (0.970)
  local copies, waits for them, and re-layouts: 5.43 us -> 2.38 us
  Pallas kernels: 47.1 us -> 48 us
    unnamed x28 -> x18, local copies, waits for them, and re-layouts: 5.43 us -> 2.38 us
    pallas_call x1, Pallas kernels: 33.9 us -> 35.2 us  [body(): pl.pallas_call(functools.partial(solve_kernel, fronts), out_shape=jax.Sha...]
where the time goes in v4:
time: 51.9 us; the launch traced here: 51.2 us
  Pallas kernels  48 us (92%)
  local copies, waits for them, and re-layouts  2.38 us (5%)
  between operations  0.77 us (1%)
    pallas_call x1, Pallas kernels, body(): pl.pallas_call(functools.partial(solve_kernel, fronts), out_shape=jax.Sha...  35.2 us
    pallas_call x1, Pallas kernels, body(): pl.pallas_call(functools.partial(pool_kernel, fronts), out_shape=(jax.Sha...  12.8 us
    unnamed x18, local copies, waits for them, and re-layouts  2.38 us

profile of v4, /device:TPU:0, one launch (start us, length us, event | category | flops | bytes accessed | tf_op | source)
XLA Modules:
  0.0 51.2 jit_solution(6428381910890964688)
XLA Ops:
  0.6 0.0 copy-start.1
  0.6 0.0 copy-start.2
  0.7 0.0 copy-start.3
  0.7 0.0 copy-start.4
  0.7 0.0 copy-start.5
  0.7 0.0 copy-start.6
  0.7 0.0 copy-start.7
  0.7 35.2 %solve.1.joined_in = f32[1024,128]{1,0:T(8,128)} custom-call(f32[512,128]{1,0:T(8,128)} %inj.1, s32[2,128]{1,0:T(2,128)} %sw_from.1, s32[2,128]{1,0:T(2,128)} %sw_to.1, f32[2,128]{1,0:T(2,128)} %sw_susc.1, f32[512,512]{1,0:T(8,128)} %coupling.1, f32[512,512]{1,0:T(8,128)} %pivot.1), custom_call_target="tpu_custom_call" | custom-call | tf_op jit(solution)/shard_map/solve/pallas_call | solution.py:498
  35.9 0.0 copy-done.1
  35.9 0.0 copy-done.2
  36.0 0.0 copy-done.3
  36.0 0.0 copy-done.4
  36.0 0.0 copy-done.5
  36.0 0.0 copy-done.6
  36.0 0.0 copy-done.7
  36.0 0.0 copy-start
  36.0 1.0 %copy-done = f32[1024,128]{1,0:T(8,128)S(1)} copy-done((f32[1024,128]{1,0:T(8,128)S(1)}, f32[1024,128]{1,0:T(8,128)}, u32[]{:S(2)}) %copy-start) | copy-done | bytes 524312
  37.0 12.8 %pool.1 = (bf16[128,128]{1,0:T(8,128)(2,1)S(1)}, f32[512,128]{1,0:T(8,128)S(1)}) custom-call(s32[512]{0:T(512)S(1)} %copy-done.2, s32[512]{0:T(512)S(1)} %copy-done.3, f32[512]{0:T(512)S(1)} %copy-done.4, s32[1,512]{1,0:T(1,128)S(1)} %bitcast.5, f32[1024,128]{1,0:T(8,128)S(1)} %copy-done, f32[1,128]{1,0:T(1,128)S(1)} %bitcast.6, f32[1,128]{1,0:T(1,128)S(1)} %bitcast.7, ...), custom_call_target="tpu_custom_call" | custom-call | tf_op jit(solution)/shard_map/pool/pallas_call | solution.py:520
  49.8 0.6 %copy.17 = bf16[1,128,128]{2,1,0:T(8,128)(2,1)} copy(bf16[1,128,128]{2,1,0:T(8,128)(2,1)S(1)} %bitcast.4) | data formatting | bytes 65536
  50.5 0.7 %copy.18 = f32[512,128]{1,0:T(8,128)} copy(f32[512,128]{1,0:T(8,128)S(1)} %get-tuple-element.9) | data formatting | bytes 524288
Async XLA Ops:
  0.6 35.3 %copy-start.1 = (bf16[128,128]{1,0:T(8,128)(2,1)S(1)}, bf16[128,128]{1,0:T(8,128)(2,1)}, u32[]{:S(2)}) copy-start(bf16[128,128]{1,0:T(8,128)(2,1)} %out_weight.1) | copy-start | bytes 98308
  0.6 35.3 %copy-start.2 = (s32[512]{0:T(512)S(1)}, s32[512]{0:T(512)}, u32[]{:S(2)}) copy-start(s32[512]{0:T(512)} %from_in.1) | copy-start | bytes 6148
  0.7 35.3 %copy-start.3 = (s32[512]{0:T(512)S(1)}, s32[512]{0:T(512)}, u32[]{:S(2)}) copy-start(s32[512]{0:T(512)} %to_in.1) | copy-start | bytes 6148
  0.7 35.3 %copy-start.4 = (f32[512]{0:T(512)S(1)}, f32[512]{0:T(512)}, u32[]{:S(2)}) copy-start(f32[512]{0:T(512)} %susc_in.1) | copy-start | bytes 6148
  0.7 35.3 %copy-start.5 = (s32[512,1]{0,1:T(1,128)S(1)}, s32[512,1]{0,1:T(1,128)}, u32[]{:S(2)}) copy-start(s32[512,1]{0,1:T(1,128)} %param.22) | copy-start | bytes 6148
  0.7 35.3 %copy-start.6 = (f32[128]{0:T(128)S(1)}, f32[128]{0:T(128)}, u32[]{:S(2)}) copy-start(f32[128]{0:T(128)} %param.23) | copy-start | bytes 1540
  0.7 35.3 %copy-start.7 = (f32[128]{0:T(128)S(1)}, f32[128]{0:T(128)}, u32[]{:S(2)}) copy-start(f32[128]{0:T(128)} %param.24) | copy-start | bytes 1540
  36.0 1.0 %copy-start = (f32[1024,128]{1,0:T(8,128)S(1)}, f32[1024,128]{1,0:T(8,128)}, u32[]{:S(2)}) copy-start(f32[1024,128]{1,0:T(8,128)} %solve.1.joined_in) | copy-start | bytes 1572868
